TPU v7x, 32 devices: a whole 2x2x4 slice. The times are simulated.
32 devices in a mesh: ty: 8 (over z, x), tx: 4 (over y, core).
Axes of the slice: x: 2, y: 2, z: 4, core: 2. Of those that a mesh axis runs over, the one named last changes fastest.
Arguments:
- fields: bfloat16 [2, 48, 64, 4096], P(None, None, 'ty', 'tx'), may hold values from -6 to 6
- kernel_one: bfloat16 [3, 3, 48, 32], replicated, may hold values from -0.3125 to 0.3125
- bias_one: float32 [32], replicated, may hold values from -1.5 to 1.5
- kernel_two: bfloat16 [3, 3, 32, 64], replicated, may hold values from -0.75 to 0.75
- bias_two: float32 [64], replicated, may hold values from -1.5 to 1.5
- kernel_three: bfloat16 [3, 3, 64, 128], replicated, may hold values from -0.5 to 0.5
- bias_three: float32 [128], replicated, may hold values from -1.5 to 1.5
- kernel_coarse: bfloat16 [3, 3, 128, 256], replicated, may hold values from -0.375 to 0.375
- bias_coarse: float32 [256], replicated, may hold values from -1.5 to 1.5
- decode_three: bfloat16 [3, 3, 384, 128], replicated, may hold values from -0.15625 to 0.15625
- offset_three: float32 [128], replicated, may hold values from -1.5 to 1.5
- decode_two: bfloat16 [3, 3, 192, 64], replicated, may hold values from -0.21875 to 0.21875
- offset_two: float32 [64], replicated, may hold values from -1.5 to 1.5
- decode_one: bfloat16 [3, 3, 96, 32], replicated, may hold values from -0.3125 to 0.3125
- offset_one: float32 [32], replicated, may hold values from -1.5 to 1.5
- head_kernel: bfloat16 [32, 48], replicated, may hold values from -1 to 1
- head_offset: float32 [48], replicated, may hold values from -3 to 3
Outputs:
- corrected: float32 [2, 48, 64, 4096], P(None, None, 'ty', 'tx')
All inputs are finite; a program needn't handle non-finite values.
Results may differ from a plain program's by a relative error of at most 0.009.
Values may be sent and summed in bfloat16 or wider, within the bound.
A program may use at most 128 MiB of HBM per device.

v0:
```python
import jax
import jax.numpy as jnp
from jax import lax
from jax.sharding import PartitionSpec as P


def extended(value, sides, width):
    for axis, dim in sides:
        size, length = (lax.axis_size(axis), value.shape[dim])
        up = [(i, (i + 1) % size) for i in range(size - 1)]
        down = [(j, i) for i, j in up]
        last = lax.slice_in_dim(value, length - width, length, axis=dim)
        first = lax.slice_in_dim(value, 0, width, axis=dim)
        before = lax.ppermute(last, axis, up)
        after = lax.ppermute(first, axis, down)
        value = jnp.concatenate([before, value, after], axis=dim)
    return value


def convolve_valid(padded, kernel, offset):
    result = lax.conv_general_dilated(
        padded,
        kernel,
        (1, 1),
        "VALID",
        dimension_numbers=("NCHW", "HWIO", "NCHW"),
        preferred_element_type=jnp.float32,
    )
    return jax.nn.silu(result + offset[None, :, None, None]).astype(jnp.bfloat16)


def tile_conv(tensor, kernel, offset):
    padded = extended(tensor, (("ty", 2), ("tx", 3)), 1)
    return convolve_valid(padded, kernel, offset)


def joined_conv(tensor, kernel, offset):
    padded = extended(tensor, (("ty", 2), ("tx", 3)), 1)
    return convolve_valid(padded, kernel, offset)


def average_pool(tensor):
    shape = tensor.shape
    blocks = tensor.astype(jnp.float32).reshape(
        shape[0], shape[1], shape[2] // 2, 2, shape[3] // 2, 2
    )
    return jnp.mean(blocks, axis=(3, 5)).astype(jnp.bfloat16)


def upsample(tensor):
    return jnp.repeat(jnp.repeat(tensor, 2, axis=2), 2, axis=3)


def body(
    fields,
    kernel_one,
    bias_one,
    kernel_two,
    bias_two,
    kernel_three,
    bias_three,
    kernel_coarse,
    bias_coarse,
    decode_three,
    offset_three,
    decode_two,
    offset_two,
    decode_one,
    offset_one,
    head_kernel,
    head_offset,
):
    skip_one = tile_conv(fields, kernel_one, bias_one)
    skip_two = tile_conv(average_pool(skip_one), kernel_two, bias_two)
    skip_three = tile_conv(average_pool(skip_two), kernel_three, bias_three)
    coarse_in = average_pool(skip_three)
    padded = extended(coarse_in, (("ty", 2), ("tx", 3)), 1)
    coarse = convolve_valid(padded, kernel_coarse, bias_coarse)
    back_three = joined_conv(
        jnp.concatenate([upsample(coarse), skip_three], axis=1), decode_three, offset_three
    )
    back_two = joined_conv(
        jnp.concatenate([upsample(back_three), skip_two], axis=1), decode_two, offset_two
    )
    back_one = joined_conv(
        jnp.concatenate([upsample(back_two), skip_one], axis=1), decode_one, offset_one
    )
    projected = jnp.einsum(
        "bchw,cv->bvhw", back_one, head_kernel, preferred_element_type=jnp.float32
    )
    return fields.astype(jnp.float32) + head_offset[None, :, None, None] + projected


def solution(mesh):
    return jax.shard_map(
        body,
        mesh=mesh,
        in_specs=(
            P(None, None, "ty", "tx"),
            P(),
            P(),
            P(),
            P(),
            P(),
            P(),
            P(),
            P(),
            P(),
            P(),
            P(),
            P(),
            P(),
            P(),
            P(),
            P(),
        ),
        out_specs=P(None, None, "ty", "tx"),
        check_vma=False,
    )
```

profile of v0, /device:TPU:11, one launch (start us, length us, event | category | flops | bytes accessed | tf_op | source)
XLA Modules:
  0.0 427.8 jit_solution(9312662971753527157)
XLA Ops:
  0.0 2.7 fusion.48
  5.1 4.0 collective-permute-start
  9.1 2.3 collective-permute-done.1
  11.7 4.9 %collective-permute-done = bf16[2,48,1,1024]{3,1,2,0:T(8,128)(2,1)S(1)} collective-permute-done((bf16[2,48,1,1024]{3,1,2,0:T(8,128)(2,1)S(1)}, bf16[2,48,1,1024]{3,1,2,0:T(8,128)(2,1)S(1)}, u32[]{:S(2)}, u32[]{:S(2)}) %collective-permute-start) | collective-permute-done | bytes 196640 | tf_op jit(solution)/shard_map/ppermute | solution.py:14
  20.9 3.5 collective-permute-start.2
  26.5 2.6 collective-permute-done.2
  29.1 4.4 %collective-permute-done.3 = bf16[2,48,10,1]{3,2,1,0:T(8,128)(2,1)S(1)} collective-permute-done((bf16[2,48,10,1]{3,2,1,0:T(8,128)(2,1)S(1)}, bf16[2,48,10,1]{3,2,1,0:T(8,128)(2,1)S(1)}, u32[]{:S(2)}, u32[]{:S(2)}) %collective-permute-start.3) | collective-permute-done | bytes 1952 | tf_op jit(solution)/shard_map/ppermute | solution.py:15
  33.5 7.5 %concatenate.52 = bf16[2,48,10,1026]{3,2,1,0:T(8,128)(2,1)} concatenate(bf16[2,48,10,1]{3,2,1,0:T(8,128)(2,1)S(1)} %collective-permute-done.2, bf16[2,48,10,1024]{3,2,1,0:T(8,128)(2,1)} %copy-done.6, bf16[2,48,10,1]{3,2,1,0:T(8,128)(2,1)S(1)} %collective-permute-done.3), dimensions={3} | concatenate | bytes 3939840 | tf_op jit(solution)/shard_map/concatenate | solution.py:16
  41.0 2.4 copy.214
  43.6 6.0 %reshape.66 = bf16[48,10,2,8,129]{4,3,0,2,1:T(8,128)(2,1)} reshape(bf16[48,10,2,1032]{3,0,2,1:T(8,128)(2,1)S(1)} %pad.clone) | data formatting | bytes 3962880 | tf_op jit(solution)/shard_map/conv_general_dilated | solution.py:21
  52.3 2.8 fusion.8
  55.1 10.9 %copy.168 = bf16[48,10,2,8,131]{0,3,2,4,1:T(8,128)(2,1)} copy(bf16[48,10,2,8,131]{4,3,0,2,1:T(8,128)(2,1)} %fusion.8) | data formatting | bytes 4024320 | tf_op jit(solution)/shard_map/conv_general_dilated | solution.py:21
  66.0 13.2 %fusion.5 = f32[8,16,129,32]{3,1,2,0:T(8,128)} fusion(bf16[3,3,48,32]{2,3,1,0:T(8,128)(2,1)S(1)} %copy-done.23, bf16[48,10,2,8,131]{0,3,2,4,1:T(8,128)(2,1)} %copy.168), kind=kOutput, calls=%fused_computation.9 | convolution fusion | flops 456523776 | bytes 4153344 | tf_op jit(solution)/shard_map/conv_general_dilated | solution.py:21
  79.2 9.1 %copy.169 = f32[8,16,129,32]{2,3,1,0:T(8,128)} copy(f32[8,16,129,32]{3,1,2,0:T(8,128)} %fusion.5) | data formatting | bytes 4227072 | tf_op jit(solution)/shard_map/conv_general_dilated | solution.py:21
  88.3 3.8 multiply_convert_fusion.1
  93.4 4.3 %reshape.70 = bf16[8,2,1032,32]{2,1,3,0:T(2,128)(2,1)} reshape(bf16[8,16,129,32]{2,1,3,0:T(8,128)(2,1)S(1)} %copy.170) | data formatting | bytes 2113536 | tf_op jit(solution)/shard_map/convert_element_type | solution.py:29
  101.3 4.7 %copy.172 = f32[2,32,8,1024]{1,3,2,0:T(8,128)} copy(f32[2,32,8,1024]{3,2,1,0:T(8,128)S(1)} %fusion.30) | data formatting | bytes 4194304 | tf_op jit(solution)/shard_map/reshape | solution.py:44
  106.0 9.6 %reduce_sum.34 = f32[2,32,4,512]{1,3,2,0:T(8,128)S(1)} reduce(f32[2,32,4,2,512,2]{1,5,4,3,2,0:T(2,128)} %bitcast.130, f32[]{:T(128)} %constant.19.clone.1), dimensions={3,5}, to_apply=%region_0.1 | reduce | flops 393216 | bytes 2621444 | tf_op jit(solution)/shard_map/reduce_sum | solution.py:47
  118.7 4.3 collective-permute-start.4
  124.5 2.5 collective-permute-done.5
  130.3 3.6 collective-permute-start.6
  137.6 2.6 copy.177
  140.2 4.3 fusion.17
  153.5 2.8 reduce_sum.35
  157.5 2.8 collective-permute-start.9
  160.3 3.4 collective-permute-start.8
  164.2 2.7 collective-permute-done.8
  169.0 5.1 %collective-permute-start.10 = (bf16[2,64,4,1]{1,3,2,0:T(2,128)(2,1)S(1)}, bf16[2,64,4,1]{1,3,2,0:T(2,128)(2,1)S(1)}, u32[]{:S(2)}, u32[]{:S(2)}) collective-permute-start(bf16[2,64,4,1]{1,3,2,0:T(2,128)(2,1)S(1)} %get-tuple-element.23), channel_id=1, source_target_pairs={{0,1},{1,2},{2,3},{4,5},{5,6},{6,7},{8,9},{9,10},{10,11},{12,13},{... | collective-permute-start | bytes 3080 | tf_op jit(solution)/shard_map/ppermute | solution.py:14
  177.5 3.3 collective-permute-start.13
  180.8 2.9 collective-permute-start.12
  187.7 5.6 %collective-permute-start.14 = (bf16[2,128,3,1]{1,3,0,2:T(2,128)(2,1)S(1)}, bf16[2,128,3,1]{1,3,0,2:T(2,128)(2,1)S(1)}, u32[]{:S(2)}, u32[]{:S(2)}) collective-permute-start(bf16[2,128,3,1]{1,3,0,2:T(2,128)(2,1)S(1)} %get-tuple-element.29), channel_id=1, source_target_pairs={{0,1},{1,2},{2,3},{4,5},{5,6},{6,7},{8,9},{9,10},{10,11},{12,13},{... | collective-permute-start | bytes 4616 | tf_op jit(solution)/shard_map/ppermute | solution.py:14
  197.7 2.5 collective-permute-start.17
  200.2 3.6 collective-permute-start.16
  203.9 11.3 %collective-permute-done.17 = bf16[2,384,1,256]{1,0,3,2:T(2,128)(2,1)S(1)} collective-permute-done((bf16[2,384,1,256]{1,0,3,2:T(2,128)(2,1)S(1)}, bf16[2,384,1,256]{1,0,3,2:T(2,128)(2,1)S(1)}, u32[]{:S(2)}, u32[]{:S(2)}) %collective-permute-start.17) | collective-permute-done | bytes 393248 | tf_op jit(solution)/shard_map/ppermute | solution.py:15
  219.6 5.3 %collective-permute-start.18 = (bf16[2,384,4,1]{1,0,3,2:T(2,128)(2,1)S(1)}, bf16[2,384,4,1]{1,0,3,2:T(2,128)(2,1)S(1)}, u32[]{:S(2)}, u32[]{:S(2)}) collective-permute-start(bf16[2,384,4,1]{1,0,3,2:T(2,128)(2,1)S(1)} %get-tuple-element.15), channel_id=1, source_target_pairs={{0,1},{1,2},{2,3},{4,5},{5,6},{6,7},{8,9},{9,10},{10,11},{12,13},{... | collective-permute-start | bytes 18440 | tf_op jit(solution)/shard_map/ppermute | solution.py:14
  225.6 4.6 %maximum_bitcast_fusion.1 = bf16[384,4,2,258]{0,2,3,1:T(2,128)(2,1)S(1)} fusion(bf16[2,384,4,1]{1,0,3,2:T(2,128)(2,1)S(1)} %collective-permute-done.19, bf16[2,384,1,256]{1,0,3,2:T(2,128)(2,1)} %copy-done.11, bf16[2,128,2,256]{1,0,3,2:T(2,128)(2,1)S(1)} %copy.190, bf16[2,256,2,256]{1,0,3,2:T(2,128)(2,1)S(1)} %broadcast_in_dim.30, ...), kind=kLoop, calls=%fused_computation.38 | loop fusion | flops 9510912 | bytes 3170304 | tf_op jit(solution)/shard_map/concatenate | solution.py:16
  238.4 4.3 collective-permute-start.20
  242.7 16.2 %collective-permute-done.21 = bf16[2,192,1,512]{1,3,2,0:T(8,128)(2,1)S(1)} collective-permute-done((bf16[2,192,1,512]{1,3,2,0:T(8,128)(2,1)S(1)}, bf16[2,192,1,512]{1,3,2,0:T(8,128)(2,1)S(1)}, u32[]{:S(2)}, u32[]{:S(2)}) %collective-permute-start.21) | collective-permute-done | bytes 393248 | tf_op jit(solution)/shard_map/ppermute | solution.py:15
  258.9 3.3 collective-permute-done.20
  264.5 4.7 %collective-permute-start.22 = (bf16[2,192,6,1]{1,3,2,0:T(2,128)(2,1)S(1)}, bf16[2,192,6,1]{1,3,2,0:T(2,128)(2,1)S(1)}, u32[]{:S(2)}, u32[]{:S(2)}) collective-permute-start(bf16[2,192,6,1]{1,3,2,0:T(2,128)(2,1)S(1)} %get-tuple-element.9), channel_id=1, source_target_pairs={{0,1},{1,2},{2,3},{4,5},{5,6},{6,7},{8,9},{9,10},{10,11},{12,13},{... | collective-permute-start | bytes 13832 | tf_op jit(solution)/shard_map/ppermute | solution.py:14
  269.2 7.2 %copy.221 = bf16[8,2,1024,32]{3,0,2,1:T(8,128)(2,1)} copy(bf16[8,2,1024,32]{2,1,3,0:T(2,128)(2,1)} %copy-done.9) | data formatting | bytes 2097152 | tf_op jit(solution)/shard_map/convert_element_type | solution.py:29
  277.8 2.4 copy.218
  280.3 2.8 pad.10.clone
  283.2 3.7 fusion.9
  286.9 6.7 %fusion.10 = f32[4,16,65,64]{3,1,2,0:T(8,128)} fusion(bf16[3,3,192,64]{2,3,1,0:T(8,128)(2,1)S(1)} %copy-done.21, bf16[192,6,2,8,67]{0,2,4,3,1:T(2,128)(2,1)S(1)} %fusion.9), kind=kOutput, calls=%fused_computation.17 | convolution fusion | flops 920125440 | bytes 3756032 | tf_op jit(solution)/shard_map/conv_general_dilated | solution.py:21
  302.9 3.1 copy-done.2
  306.0 4.8 %fusion.28 = (bf16[2,96,1,1024]{1,2,3,0:T(2,128)(2,1)S(1)}, bf16[2,96,1,1024]{1,2,3,0:T(2,128)(2,1)S(1)}) fusion(bf16[2,64,8,1024]{1,2,3,0:T(8,128)(2,1)S(1)} %bitcast.128, bf16[2,32,8,1024]{1,2,3,0:T(8,128)(2,1)S(1)} %bitcast.127), kind=kLoop, calls=%fused_computation.47 | loop fusion | flops 1572864 | bytes 3932160 | tf_op jit(solution)/shard_map/concatenate | solution.py:86
  314.1 4.3 collective-permute-start.24
  318.4 6.0 %pad_maximum_fusion.1 = bf16[2,96,8,1024]{1,2,3,0:T(8,128)(2,1)} fusion(bf16[2,32,8,1024]{1,2,3,0:T(8,128)(2,1)} %bitcast.126, bf16[2,64,8,1024]{1,2,3,0:T(8,128)(2,1)} %bitcast.129), kind=kLoop, calls=%fused_computation.22 | loop fusion | flops 6291456 | bytes 6291456 | tf_op jit(solution)/shard_map/concatenate | solution.py:86
  324.4 6.4 %copy.203 = bf16[2,96,8,1024]{3,1,2,0:T(8,128)(2,1)} copy(bf16[2,96,8,1024]{1,2,3,0:T(8,128)(2,1)} %pad_maximum_fusion.1) | data formatting | bytes 6291456 | tf_op jit(solution)/shard_map/concatenate | solution.py:86
  336.5 3.3 collective-permute-start.26
  341.8 3.8 collective-permute-done.26
  345.6 4.4 %collective-permute-done.27 = bf16[2,96,10,1]{3,1,2,0:T(8,128)(2,1)S(1)} collective-permute-done((bf16[2,96,10,1]{3,1,2,0:T(8,128)(2,1)S(1)}, bf16[2,96,10,1]{3,1,2,0:T(8,128)(2,1)S(1)}, u32[]{:S(2)}, u32[]{:S(2)}) %collective-permute-start.27) | collective-permute-done | bytes 3872 | tf_op jit(solution)/shard_map/ppermute | solution.py:15
  350.0 9.1 %concatenate.67 = bf16[2,96,10,1026]{3,1,2,0:T(8,128)(2,1)} concatenate(bf16[2,96,10,1]{3,1,2,0:T(8,128)(2,1)S(1)} %collective-permute-done.26, bf16[2,96,10,1024]{3,1,2,0:T(8,128)(2,1)} %copy-done.5, bf16[2,96,10,1]{3,1,2,0:T(8,128)(2,1)S(1)} %collective-permute-done.27), dimensions={3} | concatenate | bytes 7879680 | tf_op jit(solution)/shard_map/concatenate | solution.py:16
  359.1 8.1 %copy.219 = bf16[96,10,2,1026]{0,3,2,1:T(8,128)(2,1)} copy(bf16[96,10,2,1026]{3,0,1,2:T(8,128)(2,1)} %bitcast.131) | data formatting | bytes 7879680
  367.3 5.9 %pad.12.clone = bf16[96,10,2,1032]{0,3,2,1:T(8,128)(2,1)} pad(bf16[96,10,2,1026]{0,3,2,1:T(8,128)(2,1)} %copy.219, bf16[]{:T(256)} %constant.21), padding=0_0x0_0x0_0x0_6 | pad | bytes 7902722 | tf_op jit(solution)/shard_map/concatenate | solution.py:16
  373.2 8.4 %reshape.108 = bf16[96,10,2,8,129]{0,4,3,2,1:T(8,128)(2,1)} reshape(bf16[96,10,2,1032]{0,3,2,1:T(8,128)(2,1)} %pad.12.clone) | data formatting | bytes 7925760 | tf_op jit(solution)/shard_map/conv_general_dilated | solution.py:21
  382.6 4.2 fusion.2
  386.8 12.2 %fusion.3 = f32[8,16,129,32]{3,1,2,0:T(8,128)} fusion(bf16[3,3,96,32]{2,3,1,0:T(8,128)(2,1)S(1)} %copy-done.25, bf16[96,10,2,8,131]{0,4,3,2,1:T(8,128)(2,1)S(1)} %fusion.2), kind=kOutput, calls=%fused_computation.7 | convolution fusion | flops 913047552 | bytes 6193152 | tf_op jit(solution)/shard_map/conv_general_dilated | solution.py:21
  399.0 9.3 %copy.206 = f32[8,16,129,32]{2,3,1,0:T(8,128)} copy(f32[8,16,129,32]{3,1,2,0:T(8,128)} %fusion.3) | data formatting | bytes 4227072 | tf_op jit(solution)/shard_map/conv_general_dilated | solution.py:21
  408.3 3.8 multiply_convert_fusion
  412.1 2.6 copy.207
  414.7 5.7 %reshape.112 = bf16[8,2,1032,32]{2,1,3,0:T(2,128)(2,1)} reshape(bf16[8,16,129,32]{2,1,3,0:T(8,128)(2,1)} %copy.207) | data formatting | bytes 2113536 | tf_op jit(solution)/shard_map/convert_element_type | solution.py:29
  424.1 3.5 copy.209
  (180 shorter events, 93.8 us)
Async XLA Ops:
  0.0 233.1 %copy-start = (bf16[3,3,384,128]{3,2,1,0:T(8,128)(2,1)S(1)}, bf16[3,3,384,128]{3,2,1,0:T(8,128)(2,1)}, u32[]{:S(2)}) copy-start(bf16[3,3,384,128]{3,2,1,0:T(8,128)(2,1)} %param.26) | copy-start | bytes 2654212
  0.0 17.0 %copy-start.7 = (bf16[2,48,8,1024]{3,2,1,0:T(8,128)(2,1)S(1)}, bf16[2,48,8,1024]{3,2,1,0:T(8,128)(2,1)}, u32[]{:S(2)}) copy-start(bf16[2,48,8,1024]{3,2,1,0:T(8,128)(2,1)} %param.17) | copy-start | bytes 4718596
  2.8 8.6 %collective-permute-start.1 = (bf16[2,48,1,1024]{3,1,2,0:T(8,128)(2,1)S(1)}, bf16[2,48,1,1024]{3,1,2,0:T(8,128)(2,1)S(1)}, u32[]{:S(2)}, u32[]{:S(2)}) collective-permute-start(bf16[2,48,1,1024]{3,1,2,0:T(8,128)(2,1)S(1)} %copy.259), channel_id=1, source_target_pairs={{4,0},{8,4},{12,8},{16,12},{20,16},{24,20},{28,24},{5,1},{9,5},{13... | collective-permute-start | bytes 589832 | tf_op jit(solution)/shard_map/ppermute | solution.py:15
  5.1 11.6 %collective-permute-start = (bf16[2,48,1,1024]{3,1,2,0:T(8,128)(2,1)S(1)}, bf16[2,48,1,1024]{3,1,2,0:T(8,128)(2,1)S(1)}, u32[]{:S(2)}, u32[]{:S(2)}) collective-permute-start(bf16[2,48,1,1024]{3,1,2,0:T(8,128)(2,1)S(1)} %copy.260), channel_id=1, source_target_pairs={{0,4},{4,8},{8,12},{12,16},{16,20},{20,24},{24,28},{1,5},{5,9},{9,... | collective-permute-start | bytes 589832 | tf_op jit(solution)/shard_map/ppermute | solution.py:14
  19.0 1.7 copy-start.6
  20.9 8.2 %collective-permute-start.2 = (bf16[2,48,10,1]{3,2,1,0:T(8,128)(2,1)S(1)}, bf16[2,48,10,1]{3,2,1,0:T(8,128)(2,1)S(1)}, u32[]{:S(2)}, u32[]{:S(2)}) collective-permute-start(bf16[2,48,10,1]{3,2,1,0:T(8,128)(2,1)S(1)} %get-tuple-element.12), channel_id=1, source_target_pairs={{0,1},{1,2},{2,3},{4,5},{5,6},{6,7},{8,9},{9,10},{10,11},{12,13},{... | collective-permute-start | bytes 5768 | tf_op jit(solution)/shard_map/ppermute | solution.py:14
  24.4 9.1 %collective-permute-start.3 = (bf16[2,48,10,1]{3,2,1,0:T(8,128)(2,1)S(1)}, bf16[2,48,10,1]{3,2,1,0:T(8,128)(2,1)S(1)}, u32[]{:S(2)}, u32[]{:S(2)}) collective-permute-start(bf16[2,48,10,1]{3,2,1,0:T(8,128)(2,1)S(1)} %get-tuple-element.11), channel_id=1, source_target_pairs={{1,0},{2,1},{3,2},{5,4},{6,5},{7,6},{9,8},{10,9},{11,10},{13,12},{... | collective-permute-start | bytes 5768 | tf_op jit(solution)/shard_map/ppermute | solution.py:15
  49.6 2.7 copy-start.4
  55.1 10.9 %copy-start.23 = (bf16[3,3,48,32]{2,3,1,0:T(8,128)(2,1)S(1)}, bf16[3,3,48,32]{2,3,1,0:T(8,128)(2,1)}, u32[]{:S(2)}) copy-start(bf16[3,3,48,32]{2,3,1,0:T(8,128)(2,1)} %param.18) | copy-start | bytes 82948
  79.2 9.1 %copy-start.13 = (pred[16,129]{1,0:T(8,128)(4,1)S(1)}, pred[16,129]{1,0:T(8,128)(4,1)}, u32[]{:S(2)}) copy-start(pred[16,129]{1,0:T(8,128)(4,1)} %constant.49) | copy-start | bytes 6196
  79.2 9.1 %copy-start.17 = (f32[32]{0:T(128)S(1)}, f32[32]{0:T(128)}, u32[]{:S(2)}) copy-start(f32[32]{0:T(128)} %param.19) | copy-start | bytes 388
  99.7 1.0 copy-start.9
  115.8 1.0 copy-start.10
  116.8 10.3 %collective-permute-start.5 = (bf16[2,32,1,512]{1,3,2,0:T(8,128)(2,1)S(1)}, bf16[2,32,1,512]{1,3,2,0:T(8,128)(2,1)S(1)}, u32[]{:S(2)}, u32[]{:S(2)}) collective-permute-start(bf16[2,32,1,512]{1,3,2,0:T(8,128)(2,1)S(1)} %get-tuple-element.20), channel_id=1, source_target_pairs={{4,0},{8,4},{12,8},{16,12},{20,16},{24,20},{28,24},{5,1},{9,5},{13... | collective-permute-start | bytes 196616 | tf_op jit(solution)/shard_map/ppermute | solution.py:15
  118.7 9.5 %collective-permute-start.4 = (bf16[2,32,1,512]{1,3,2,0:T(8,128)(2,1)S(1)}, bf16[2,32,1,512]{1,3,2,0:T(8,128)(2,1)S(1)}, u32[]{:S(2)}, u32[]{:S(2)}) collective-permute-start(bf16[2,32,1,512]{1,3,2,0:T(8,128)(2,1)S(1)} %get-tuple-element.19), channel_id=1, source_target_pairs={{0,4},{4,8},{8,12},{12,16},{16,20},{20,24},{24,28},{1,5},{5,9},{9,... | collective-permute-start | bytes 196616 | tf_op jit(solution)/shard_map/ppermute | solution.py:14
  128.4 5.9 %collective-permute-start.7 = (bf16[2,32,6,1]{3,1,2,0:T(8,128)(2,1)S(1)}, bf16[2,32,6,1]{3,1,2,0:T(8,128)(2,1)S(1)}, u32[]{:S(2)}, u32[]{:S(2)}) collective-permute-start(bf16[2,32,6,1]{3,1,2,0:T(8,128)(2,1)S(1)} %get-tuple-element.26), channel_id=1, source_target_pairs={{1,0},{2,1},{3,2},{5,4},{6,5},{7,6},{9,8},{10,9},{11,10},{13,12},{... | collective-permute-start | bytes 2312 | tf_op jit(solution)/shard_map/ppermute | solution.py:15
  130.3 5.3 %collective-permute-start.6 = (bf16[2,32,6,1]{3,1,2,0:T(8,128)(2,1)S(1)}, bf16[2,32,6,1]{3,1,2,0:T(8,128)(2,1)S(1)}, u32[]{:S(2)}, u32[]{:S(2)}) collective-permute-start(bf16[2,32,6,1]{3,1,2,0:T(8,128)(2,1)S(1)} %get-tuple-element.25), channel_id=1, source_target_pairs={{0,1},{1,2},{2,3},{4,5},{5,6},{6,7},{8,9},{9,10},{10,11},{12,13},{... | collective-permute-start | bytes 2312 | tf_op jit(solution)/shard_map/ppermute | solution.py:14
  136.8 3.4 copy-start.24
  144.5 2.2 copy-start.15
  144.5 2.2 copy-start.18
  156.4 19.9 %copy-start.22 = (bf16[3,3,64,128]{3,2,1,0:T(8,128)(2,1)S(1)}, bf16[3,3,64,128]{3,2,1,0:T(8,128)(2,1)}, u32[]{:S(2)}) copy-start(bf16[3,3,64,128]{3,2,1,0:T(8,128)(2,1)} %param.22) | copy-start | bytes 442372
  156.4 19.9 %copy-start.27 = (f32[128]{0:T(128)S(1)}, f32[128]{0:T(128)}, u32[]{:S(2)}) copy-start(f32[128]{0:T(128)} %param.23) | copy-start | bytes 1540
  156.4 19.9 %copy-start.29 = (pred[16,33]{0,1:T(8,128)(4,1)S(1)}, pred[16,33]{0,1:T(8,128)(4,1)}, u32[]{:S(2)}) copy-start(pred[16,33]{0,1:T(8,128)(4,1)} %constant.51) | copy-start | bytes 1588
  157.5 6.7 %collective-permute-start.9 = (bf16[2,64,1,256]{1,3,2,0:T(8,128)(2,1)S(1)}, bf16[2,64,1,256]{1,3,2,0:T(8,128)(2,1)S(1)}, u32[]{:S(2)}, u32[]{:S(2)}) collective-permute-start(bf16[2,64,1,256]{1,3,2,0:T(8,128)(2,1)S(1)} %get-tuple-element.28), channel_id=1, source_target_pairs={{4,0},{8,4},{12,8},{16,12},{20,16},{24,20},{28,24},{5,1},{9,5},{13... | collective-permute-start | bytes 196616 | tf_op jit(solution)/shard_map/ppermute | solution.py:15
  160.3 6.6 %collective-permute-start.8 = (bf16[2,64,1,256]{1,3,2,0:T(8,128)(2,1)S(1)}, bf16[2,64,1,256]{1,3,2,0:T(8,128)(2,1)S(1)}, u32[]{:S(2)}, u32[]{:S(2)}) collective-permute-start(bf16[2,64,1,256]{1,3,2,0:T(8,128)(2,1)S(1)} %get-tuple-element.27), channel_id=1, source_target_pairs={{0,4},{4,8},{8,12},{12,16},{16,20},{20,24},{24,28},{1,5},{5,9},{9,... | collective-permute-start | bytes 196616 | tf_op jit(solution)/shard_map/ppermute | solution.py:14
  167.0 7.2 %collective-permute-start.11 = (bf16[2,64,4,1]{1,3,2,0:T(2,128)(2,1)S(1)}, bf16[2,64,4,1]{1,3,2,0:T(2,128)(2,1)S(1)}, u32[]{:S(2)}, u32[]{:S(2)}) collective-permute-start(bf16[2,64,4,1]{1,3,2,0:T(2,128)(2,1)S(1)} %get-tuple-element.24), channel_id=1, source_target_pairs={{1,0},{2,1},{3,2},{5,4},{6,5},{7,6},{9,8},{10,9},{11,10},{13,12},{... | collective-permute-start | bytes 3080 | tf_op jit(solution)/shard_map/ppermute | solution.py:15
  169.0 5.4 %collective-permute-start.10 = (bf16[2,64,4,1]{1,3,2,0:T(2,128)(2,1)S(1)}, bf16[2,64,4,1]{1,3,2,0:T(2,128)(2,1)S(1)}, u32[]{:S(2)}, u32[]{:S(2)}) collective-permute-start(bf16[2,64,4,1]{1,3,2,0:T(2,128)(2,1)S(1)} %get-tuple-element.23), channel_id=1, source_target_pairs={{0,1},{1,2},{2,3},{4,5},{5,6},{6,7},{8,9},{9,10},{10,11},{12,13},{... | collective-permute-start | bytes 3080 | tf_op jit(solution)/shard_map/ppermute | solution.py:14
  176.9 17.8 %copy-start.26 = (f32[256]{0:T(256)S(1)}, f32[256]{0:T(256)}, u32[]{:S(2)}) copy-start(f32[256]{0:T(256)} %param.25) | copy-start | bytes 3076
  177.0 17.7 %copy-start.30 = (pred[16,17]{0,1:T(8,128)(4,1)S(1)}, pred[16,17]{0,1:T(8,128)(4,1)}, u32[]{:S(2)}) copy-start(pred[16,17]{0,1:T(8,128)(4,1)} %constant.52) | copy-start | bytes 820
  177.5 6.5 %collective-permute-start.13 = (bf16[2,128,1,128]{1,3,0,2:T(8,128)(2,1)S(1)}, bf16[2,128,1,128]{1,3,0,2:T(8,128)(2,1)S(1)}, u32[]{:S(2)}, u32[]{:S(2)}) collective-permute-start(bf16[2,128,1,128]{1,3,0,2:T(8,128)(2,1)S(1)} %fusion.44), channel_id=1, source_target_pairs={{4,0},{8,4},{12,8},{16,12},{20,16},{24,20},{28,24},{5,1},{9,5},{13... | collective-permute-start | bytes 196616 | tf_op jit(solution)/shard_map/ppermute | solution.py:15
  180.8 5.0 %collective-permute-start.12 = (bf16[2,128,1,128]{1,3,0,2:T(8,128)(2,1)S(1)}, bf16[2,128,1,128]{1,3,0,2:T(8,128)(2,1)S(1)}, u32[]{:S(2)}, u32[]{:S(2)}) collective-permute-start(bf16[2,128,1,128]{1,3,0,2:T(8,128)(2,1)S(1)} %fusion.44), channel_id=1, source_target_pairs={{0,4},{4,8},{8,12},{12,16},{16,20},{20,24},{24,28},{1,5},{5,9},{9,... | collective-permute-start | bytes 196616 | tf_op jit(solution)/shard_map/ppermute | solution.py:14
  185.8 8.0 %collective-permute-start.15 = (bf16[2,128,3,1]{1,3,0,2:T(2,128)(2,1)S(1)}, bf16[2,128,3,1]{1,3,0,2:T(2,128)(2,1)S(1)}, u32[]{:S(2)}, u32[]{:S(2)}) collective-permute-start(bf16[2,128,3,1]{1,3,0,2:T(2,128)(2,1)S(1)} %get-tuple-element.30), channel_id=1, source_target_pairs={{1,0},{2,1},{3,2},{5,4},{6,5},{7,6},{9,8},{10,9},{11,10},{13,12},{... | collective-permute-start | bytes 4616 | tf_op jit(solution)/shard_map/ppermute | solution.py:15
  187.7 6.3 %collective-permute-start.14 = (bf16[2,128,3,1]{1,3,0,2:T(2,128)(2,1)S(1)}, bf16[2,128,3,1]{1,3,0,2:T(2,128)(2,1)S(1)}, u32[]{:S(2)}, u32[]{:S(2)}) collective-permute-start(bf16[2,128,3,1]{1,3,0,2:T(2,128)(2,1)S(1)} %get-tuple-element.29), channel_id=1, source_target_pairs={{0,1},{1,2},{2,3},{4,5},{5,6},{6,7},{8,9},{9,10},{10,11},{12,13},{... | collective-permute-start | bytes 4616 | tf_op jit(solution)/shard_map/ppermute | solution.py:14
  197.7 17.5 %collective-permute-start.17 = (bf16[2,384,1,256]{1,0,3,2:T(2,128)(2,1)S(1)}, bf16[2,384,1,256]{1,0,3,2:T(2,128)(2,1)S(1)}, u32[]{:S(2)}, u32[]{:S(2)}) collective-permute-start(bf16[2,384,1,256]{1,0,3,2:T(2,128)(2,1)S(1)} %get-tuple-element.22), channel_id=1, source_target_pairs={{4,0},{8,4},{12,8},{16,12},{20,16},{24,20},{28,24},{5,1},{9,5},{13... | collective-permute-start | bytes 1179656 | tf_op jit(solution)/shard_map/ppermute | solution.py:15
  200.2 17.0 %collective-permute-start.16 = (bf16[2,384,1,256]{1,0,3,2:T(2,128)(2,1)S(1)}, bf16[2,384,1,256]{1,0,3,2:T(2,128)(2,1)S(1)}, u32[]{:S(2)}, u32[]{:S(2)}) collective-permute-start(bf16[2,384,1,256]{1,0,3,2:T(2,128)(2,1)S(1)} %get-tuple-element.21), channel_id=1, source_target_pairs={{0,4},{4,8},{8,12},{12,16},{16,20},{20,24},{24,28},{1,5},{5,9},{9,... | collective-permute-start | bytes 1179656 | tf_op jit(solution)/shard_map/ppermute | solution.py:14
  215.2 4.4 %copy-start.11 = (bf16[2,384,1,256]{1,0,3,2:T(2,128)(2,1)}, bf16[2,384,1,256]{1,0,3,2:T(2,128)(2,1)S(1)}, u32[]{:S(2)}) copy-start(bf16[2,384,1,256]{1,0,3,2:T(2,128)(2,1)S(1)} %collective-permute-done.17) | copy-start | bytes 1179652
  217.3 2.3 copy-start.12
  217.3 8.3 %collective-permute-start.19 = (bf16[2,384,4,1]{1,0,3,2:T(2,128)(2,1)S(1)}, bf16[2,384,4,1]{1,0,3,2:T(2,128)(2,1)S(1)}, u32[]{:S(2)}, u32[]{:S(2)}) collective-permute-start(bf16[2,384,4,1]{1,0,3,2:T(2,128)(2,1)S(1)} %get-tuple-element.16), channel_id=1, source_target_pairs={{1,0},{2,1},{3,2},{5,4},{6,5},{7,6},{9,8},{10,9},{11,10},{13,12},{... | collective-permute-start | bytes 18440 | tf_op jit(solution)/shard_map/ppermute | solution.py:15
  219.6 6.0 %collective-permute-start.18 = (bf16[2,384,4,1]{1,0,3,2:T(2,128)(2,1)S(1)}, bf16[2,384,4,1]{1,0,3,2:T(2,128)(2,1)S(1)}, u32[]{:S(2)}, u32[]{:S(2)}) collective-permute-start(bf16[2,384,4,1]{1,0,3,2:T(2,128)(2,1)S(1)} %get-tuple-element.15), channel_id=1, source_target_pairs={{0,1},{1,2},{2,3},{4,5},{5,6},{6,7},{8,9},{9,10},{10,11},{12,13},{... | collective-permute-start | bytes 18440 | tf_op jit(solution)/shard_map/ppermute | solution.py:14
  230.1 2.9 copy-start.28
  236.5 22.4 %collective-permute-start.21 = (bf16[2,192,1,512]{1,3,2,0:T(8,128)(2,1)S(1)}, bf16[2,192,1,512]{1,3,2,0:T(8,128)(2,1)S(1)}, u32[]{:S(2)}, u32[]{:S(2)}) collective-permute-start(bf16[2,192,1,512]{1,3,2,0:T(8,128)(2,1)S(1)} %get-tuple-element.14), channel_id=1, source_target_pairs={{4,0},{8,4},{12,8},{16,12},{20,16},{24,20},{28,24},{5,1},{9,5},{13... | collective-permute-start | bytes 1179656 | tf_op jit(solution)/shard_map/ppermute | solution.py:15
  238.4 23.7 %collective-permute-start.20 = (bf16[2,192,1,512]{1,3,2,0:T(8,128)(2,1)S(1)}, bf16[2,192,1,512]{1,3,2,0:T(8,128)(2,1)S(1)}, u32[]{:S(2)}, u32[]{:S(2)}) collective-permute-start(bf16[2,192,1,512]{1,3,2,0:T(8,128)(2,1)S(1)} %get-tuple-element.13), channel_id=1, source_target_pairs={{0,4},{4,8},{8,12},{12,16},{16,20},{20,24},{24,28},{1,5},{5,9},{9,... | collective-permute-start | bytes 1179656 | tf_op jit(solution)/shard_map/ppermute | solution.py:14
  262.2 14.2 %collective-permute-start.23 = (bf16[2,192,6,1]{1,3,2,0:T(2,128)(2,1)S(1)}, bf16[2,192,6,1]{1,3,2,0:T(2,128)(2,1)S(1)}, u32[]{:S(2)}, u32[]{:S(2)}) collective-permute-start(bf16[2,192,6,1]{1,3,2,0:T(2,128)(2,1)S(1)} %get-tuple-element.10), channel_id=1, source_target_pairs={{1,0},{2,1},{3,2},{5,4},{6,5},{7,6},{9,8},{10,9},{11,10},{13,12},{... | collective-permute-start | bytes 13832 | tf_op jit(solution)/shard_map/ppermute | solution.py:15
  264.5 11.9 %collective-permute-start.22 = (bf16[2,192,6,1]{1,3,2,0:T(2,128)(2,1)S(1)}, bf16[2,192,6,1]{1,3,2,0:T(2,128)(2,1)S(1)}, u32[]{:S(2)}, u32[]{:S(2)}) collective-permute-start(bf16[2,192,6,1]{1,3,2,0:T(2,128)(2,1)S(1)} %get-tuple-element.9), channel_id=1, source_target_pairs={{0,1},{1,2},{2,3},{4,5},{5,6},{6,7},{8,9},{9,10},{10,11},{12,13},{... | collective-permute-start | bytes 13832 | tf_op jit(solution)/shard_map/ppermute | solution.py:14
  283.2 3.7 copy-start.21
  293.6 2.1 copy-start.19
  302.3 3.7 copy-start.2
  302.9 8.0 %copy-start.3 = (bf16[2,64,8,512,2]{1,2,4,3,0:T(8,128)(2,1)}, bf16[2,64,8,512,2]{1,2,4,3,0:T(8,128)(2,1)S(1)}, u32[]{:S(2)}) copy-start(bf16[2,64,8,512,2]{1,2,4,3,0:T(8,128)(2,1)S(1)} %broadcast_in_dim.34) | copy-start | bytes 6291460
  311.5 19.3 %collective-permute-start.25 = (bf16[2,96,1,1024]{3,1,2,0:T(8,128)(2,1)S(1)}, bf16[2,96,1,1024]{3,1,2,0:T(8,128)(2,1)S(1)}, u32[]{:S(2)}, u32[]{:S(2)}) collective-permute-start(bf16[2,96,1,1024]{3,1,2,0:T(8,128)(2,1)S(1)} %copy.202), channel_id=1, source_target_pairs={{4,0},{8,4},{12,8},{16,12},{20,16},{24,20},{28,24},{5,1},{9,5},{13... | collective-permute-start | bytes 1179656 | tf_op jit(solution)/shard_map/ppermute | solution.py:15
  314.1 18.1 %collective-permute-start.24 = (bf16[2,96,1,1024]{3,1,2,0:T(8,128)(2,1)S(1)}, bf16[2,96,1,1024]{3,1,2,0:T(8,128)(2,1)S(1)}, u32[]{:S(2)}, u32[]{:S(2)}) collective-permute-start(bf16[2,96,1,1024]{3,1,2,0:T(8,128)(2,1)S(1)} %copy.201), channel_id=1, source_target_pairs={{0,4},{4,8},{8,12},{12,16},{16,20},{20,24},{24,28},{1,5},{5,9},{9,... | collective-permute-start | bytes 1179656 | tf_op jit(solution)/shard_map/ppermute | solution.py:14
  334.4 1.9 copy-start.5
  336.5 9.1 %collective-permute-start.26 = (bf16[2,96,10,1]{3,1,2,0:T(8,128)(2,1)S(1)}, bf16[2,96,10,1]{3,1,2,0:T(8,128)(2,1)S(1)}, u32[]{:S(2)}, u32[]{:S(2)}) collective-permute-start(bf16[2,96,10,1]{3,1,2,0:T(8,128)(2,1)S(1)} %get-tuple-element.8), channel_id=1, source_target_pairs={{0,1},{1,2},{2,3},{4,5},{5,6},{6,7},{8,9},{9,10},{10,11},{12,13},{... | collective-permute-start | bytes 11528 | tf_op jit(solution)/shard_map/ppermute | solution.py:14
  339.9 10.1 %collective-permute-start.27 = (bf16[2,96,10,1]{3,1,2,0:T(8,128)(2,1)S(1)}, bf16[2,96,10,1]{3,1,2,0:T(8,128)(2,1)S(1)}, u32[]{:S(2)}, u32[]{:S(2)}) collective-permute-start(bf16[2,96,10,1]{3,1,2,0:T(8,128)(2,1)S(1)} %get-tuple-element.7), channel_id=1, source_target_pairs={{1,0},{2,1},{3,2},{5,4},{6,5},{7,6},{9,8},{10,9},{11,10},{13,12},{... | collective-permute-start | bytes 11528 | tf_op jit(solution)/shard_map/ppermute | solution.py:15
  382.6 4.2 copy-start.25
  399.0 9.3 %copy-start.20 = (f32[32]{0:T(128)S(1)}, f32[32]{0:T(128)}, u32[]{:S(2)}) copy-start(f32[32]{0:T(128)} %param.31) | copy-start | bytes 388
  414.7 7.8 %copy-start.8 = (bf16[2,48,8,1024]{3,2,1,0:T(8,128)(2,1)S(1)}, bf16[2,48,8,1024]{3,2,1,0:T(8,128)(2,1)}, u32[]{:S(2)}) copy-start(bf16[2,48,8,1024]{3,2,1,0:T(8,128)(2,1)} %param.17) | copy-start | bytes 4718596
  414.7 7.8 %copy-start.14 = (bf16[32,48]{1,0:T(8,128)(2,1)S(1)}, bf16[32,48]{1,0:T(8,128)(2,1)}, u32[]{:S(2)}) copy-start(bf16[32,48]{1,0:T(8,128)(2,1)} %param.32) | copy-start | bytes 9220
  414.7 7.8 %copy-start.16 = (f32[48]{0:T(128)S(1)}, f32[48]{0:T(128)}, u32[]{:S(2)}) copy-start(f32[48]{0:T(128)} %param.33) | copy-start | bytes 580
  422.5 5.0 %copy-start.1 = (bf16[3,3,384,128]{3,2,1,0:T(8,128)(2,1)S(1)}, bf16[3,3,384,128]{3,2,1,0:T(8,128)(2,1)}, u32[]{:S(2)}) copy-start(bf16[3,3,384,128]{3,2,1,0:T(8,128)(2,1)} %param.26) | copy-start | bytes 2654212
where the time goes:
time: 434 us; the launch traced here: 428 us
  local copies, waits for them, and re-layouts  167 us (38%)
  starting transfers between devices  89 us (21%)
  waiting for transfers between devices  67.4 us (16%)
  other arithmetic  61 us (14%)
  matrix products  42 us (10%)
    ppermute x14, starting transfers between devices, extended(): before = lax.ppermute(last, axis, up)  58 us
    conv_general_dilated x16, local copies, waits for them, and re-layouts, convolve_valid(): lax.conv_general_dilated(padded, kernel, (1, 1), 'VALID', dimension_numbe...  55 us
    ppermute x14, waiting for transfers between devices, extended(): after = lax.ppermute(first, axis, down)  42 us
    conv_general_dilated x7, matrix products, convolve_valid(): lax.conv_general_dilated(padded, kernel, (1, 1), 'VALID', dimension_numbe...  40.5 us
    convert_element_type x25, local copies, waits for them, and re-layouts, convolve_valid(): jax.nn.silu(result + offset[None, :, None, None]).astype(jnp.bfloat16)  34.9 us
    ppermute x14, starting transfers between devices, extended(): after = lax.ppermute(first, axis, down)  31.1 us
    concatenate x9, local copies, waits for them, and re-layouts, extended(): value = jnp.concatenate([before, value, after], axis=dim)  27.5 us
    ppermute x14, waiting for transfers between devices, extended(): before = lax.ppermute(last, axis, up)  25.4 us
  transfers between devices with their start and end apart: 28, of which 20 were waited for; matrix products, arithmetic and copies ran while one was open for 6% of the time, Pallas kernels for 0%

commit v1 on v0

v1 whole, which is shorter than its diff:
```python
import functools

import jax
import jax.numpy as jnp
from jax import lax
from jax.experimental import pallas as pl
from jax.experimental.pallas import tpu as pltpu
from jax.sharding import PartitionSpec as P

LANES = 128
MESH = pl.DeviceIdType.MESH


def halved(width):
    return -(-width // (2 * LANES)) * LANES


def kernel(
    sizes,
    fields,
    k1,
    k2,
    k3,
    kc,
    d3,
    d2,
    d1,
    hk,
    bias,
    out,
    f0,
    s1,
    p1,
    s2,
    p2,
    s3,
    p3,
    c4,
    u3,
    b3,
    u2,
    b2,
    u1,
    pool_m,
    up_m,
    send,
    recv,
):
    nty, ntx, offsets = sizes
    hours, rows, _, core = fields.shape
    ty, tx = lax.axis_index("ty"), lax.axis_index("tx")
    has_up, has_down = ty > 0, ty < nty - 1
    has_left, has_right = tx > 0, tx < ntx - 1
    far = LANES + core

    for buf in (f0, s1, p1, s2, p2, s3, p3, c4, b3, b2):
        edge = jnp.zeros((buf.shape[0],) + buf.shape[2:], buf.dtype)
        buf[:, 0] = edge
        buf[:, buf.shape[1] - 1] = edge
    side = jnp.zeros((hours, rows) + (f0.shape[2], LANES), f0.dtype)
    f0[:, 1 : rows + 1, :, 0:LANES] = side
    f0[:, 1 : rows + 1, :, far : far + LANES] = side

    barrier = pltpu.get_barrier_semaphore()
    sides = (
        (has_up, {"ty": ty - 1}),
        (has_down, {"ty": ty + 1}),
        (has_left, {"tx": tx - 1}),
        (has_right, {"tx": tx + 1}),
    )
    count = jnp.int32(0)
    for has, where in sides:
        count = count + jnp.where(has, 1, 0)

        @pl.when(has)
        def _():
            pl.semaphore_signal(barrier, inc=1, device_id=where, device_id_type=MESH)

    pl.semaphore_wait(barrier, count)

    def pair(slot, first, second):
        made = []
        for at, (has, other, where, src, dst) in enumerate((first, second)):
            copy = pltpu.make_async_remote_copy(
                src_ref=src,
                dst_ref=dst,
                send_sem=send.at[slot * 2 + at],
                recv_sem=recv.at[slot * 2 + at],
                device_id=where,
                device_id_type=MESH,
            )
            made.append((has, other, copy))

            @pl.when(has)
            def _():
                copy.start()

        def wait():
            for has, other, copy in made:

                @pl.when(has)
                def _():
                    copy.wait_send()

                @pl.when(other)
                def _():
                    copy.wait_recv()

        return wait

    def vertical(slot, top, bottom, after, before):
        return pair(
            slot,
            (has_up, has_down, {"ty": ty - 1}, top, after),
            (has_down, has_up, {"ty": ty + 1}, bottom, before),
        )

    def row_exchange(slot, buf):
        last = buf.shape[1] - 1
        return vertical(slot, buf.at[:, 1], buf.at[:, last - 1], buf.at[:, last], buf.at[:, 0])

    middle = pl.ds(LANES, core)
    wait_sides = pair(
        0,
        (
            has_left,
            has_right,
            {"tx": tx - 1},
            fields.at[:, :, :, pl.ds(0, LANES)],
            f0.at[:, pl.ds(1, rows), :, pl.ds(far, LANES)],
        ),
        (
            has_right,
            has_left,
            {"tx": tx + 1},
            fields.at[:, :, :, pl.ds(core - LANES, LANES)],
            f0.at[:, pl.ds(1, rows), :, pl.ds(0, LANES)],
        ),
    )
    wait_rows = vertical(
        1,
        fields.at[:, 0],
        fields.at[:, rows - 1],
        f0.at[:, rows + 1, :, middle],
        f0.at[:, 0, :, middle],
    )

    f0[:, 1 : rows + 1, :, LANES:far] = fields[...]
    two, one = 2 * LANES, LANES
    tall = lax.broadcasted_iota(jnp.int32, (two, one), 0)
    wide = lax.broadcasted_iota(jnp.int32, (two, one), 1)
    pool_m[...] = jnp.where(lax.shift_right_logical(tall, 1) == wide, 0.25, 0.0).astype(jnp.bfloat16)
    tall = lax.broadcasted_iota(jnp.int32, (one, two), 0)
    wide = lax.broadcasted_iota(jnp.int32, (one, two), 1)
    up_m[...] = jnp.where(lax.shift_right_logical(wide, 1) == tall, 1.0, 0.0).astype(jnp.bfloat16)

    wait_sides()
    waits = []
    for at, start in enumerate((0, far)):
        lanes = pl.ds(start, LANES)
        waits.append(
            vertical(
                2 + at,
                f0.at[:, 1, :, lanes],
                f0.at[:, rows, :, lanes],
                f0.at[:, rows + 1, :, lanes],
                f0.at[:, 0, :, lanes],
            )
        )
    wait_rows()
    for wait in waits:
        wait()

    def inside(width, level):
        column = lax.broadcasted_iota(jnp.int32, (1, width), 1)
        column = column + (tx * (core >> level) - (LANES >> level))
        return (column >= 0) & (column < ntx * (core >> level))

    def conv(weights, at, operand, level):
        width = operand.shape[1]
        size = weights.shape[0] // 3
        terms = jnp.dot(weights[...], operand, preferred_element_type=jnp.float32)
        total = terms[size : 2 * size] + bias[offsets[at] : offsets[at] + size]
        total = total + pltpu.roll(terms[:size], 1, 1)
        total = total + pltpu.roll(terms[2 * size :], width - 1, 1)
        half = 0.5 * total
        result = half * jnp.tanh(half) + half
        if level is not None:
            result = jnp.where(inside(width, level), result, 0.0)
        return result.astype(jnp.bfloat16)

    def pooled(first, second):
        width = first.shape[1]
        pieces = []
        for start in range(0, width, two):
            stop = min(start + two, width)
            block = pool_m[0 : stop - start]
            pieces.append(
                jnp.dot(first[:, start:stop], block, preferred_element_type=jnp.float32)
                + jnp.dot(second[:, start:stop], block, preferred_element_type=jnp.float32)
            )
        return jnp.concatenate(pieces, axis=1).astype(jnp.bfloat16)

    def widen(src, dst):
        width = dst.shape[3]
        n = src.shape[1]

        def step(index, carry):
            h, r = lax.div(index, n), lax.rem(index, n)
            for start in range(0, width, two):
                stop = min(start + two, width)
                block = src[h, r, :, start // 2 : start // 2 + one]
                dst[h, r, :, start:stop] = jnp.dot(
                    block, up_m[:, 0 : stop - start], preferred_element_type=jnp.float32
                ).astype(jnp.bfloat16)
            return carry

        lax.fori_loop(0, hours * n, step, 0)

    def taps(buf, h, r):
        block = buf[h, pl.ds(r, 3)]
        return block.reshape(3 * buf.shape[2], buf.shape[3])

    def encode(src, weights, at, dst, nxt, level):
        half = (src.shape[1] - 2) // 2

        def step(index, carry):
            h, i = lax.div(index, half), lax.rem(index, half)
            made = []
            for off in range(2):
                r = 2 * i + off
                row = conv(weights, at, taps(src, h, r), level)
                dst[h, r + 1] = row
                made.append(row)
            nxt[h, i + 1] = pooled(*made)
            return carry

        lax.fori_loop(0, hours * half, step, 0)

    def decode(up, skip, weights, at, write, level):
        half = (skip.shape[1] - 2) // 2

        def step(index, carry):
            h, i = lax.div(index, half), lax.rem(index, half)
            above, here, below = up[h, i], up[h, i + 1], up[h, i + 2]
            for off in range(2):
                r = 2 * i + off
                three = (above, here, here) if off == 0 else (here, here, below)
                operand = jnp.concatenate(three + (taps(skip, h, r),), axis=0)
                write(h, r, conv(weights, at, operand, level))
            return carry

        lax.fori_loop(0, hours * half, step, 0)

    encode(f0, k1, 0, s1, p1, 0)
    wait_p1 = row_exchange(4, p1)
    wait_s1 = row_exchange(5, s1)
    wait_p1()
    encode(p1, k2, 1, s2, p2, 1)
    wait_p2 = row_exchange(6, p2)
    wait_s2 = row_exchange(7, s2)
    wait_p2()
    encode(p2, k3, 2, s3, p3, 2)
    wait_p3 = row_exchange(8, p3)
    wait_s3 = row_exchange(9, s3)
    wait_p3()
    for h in range(hours):
        for r in range(c4.shape[1] - 2):
            c4[h, r + 1] = conv(kc, 3, taps(p3, h, r), 3)
    wait_c4 = row_exchange(10, c4)
    wait_c4()
    wait_s3()
    widen(c4, u3)

    def keep(buf):
        def write(h, r, value):
            buf[h, r + 1] = value

        return write

    decode(u3, s3, d3, 4, keep(b3), 2)
    wait_b3 = row_exchange(11, b3)
    wait_b3()
    wait_s2()
    widen(b3, u2)
    decode(u2, s2, d2, 5, keep(b2), 1)
    wait_b2 = row_exchange(12, b2)
    wait_b2()
    wait_s1()
    widen(b2, u1)

    def head(h, r, value):
        total = jnp.dot(hk[...], value[:, LANES:far], preferred_element_type=jnp.float32)
        total = total + bias[offsets[7] : offsets[7] + hk.shape[0]]
        out[h, r] = total + f0[h, r + 1, :, LANES:far].astype(jnp.float32)

    decode(u1, s1, d1, 6, head, None)


def stacked(weights, parts):
    blocks = []
    for start, stop in parts:
        block = jnp.transpose(weights[:, :, start:stop], (1, 3, 0, 2))
        blocks.append(block.reshape(3 * weights.shape[3], 3 * (stop - start)))
    return blocks[0] if len(blocks) == 1 else jnp.concatenate(blocks, axis=1)


def body(
    nty,
    ntx,
    fields,
    kernel_one,
    bias_one,
    kernel_two,
    bias_two,
    kernel_three,
    bias_three,
    kernel_coarse,
    bias_coarse,
    decode_three,
    offset_three,
    decode_two,
    offset_two,
    decode_one,
    offset_one,
    head_kernel,
    head_offset,
):
    hours, nv, rows, core = fields.shape
    biases = (
        bias_one,
        bias_two,
        bias_three,
        bias_coarse,
        offset_three,
        offset_two,
        offset_one,
        head_offset,
    )
    offsets, total = [], 0
    for item in biases:
        offsets.append(total)
        total += item.shape[0]
    bias = jnp.concatenate(biases).reshape(total, 1)
    c1, c2, c3, c4 = (k.shape[3] for k in (kernel_one, kernel_two, kernel_three, kernel_coarse))
    encoders = [
        stacked(k, ((0, k.shape[2]),))
        for k in (kernel_one, kernel_two, kernel_three, kernel_coarse)
    ]
    decoders = [
        stacked(k, ((0, cut), (cut, k.shape[2])))
        for k, cut in ((decode_three, c4), (decode_two, c3), (decode_one, c2))
    ]
    w1 = core + 2 * LANES
    w2 = halved(w1)
    w3 = halved(w2)
    w4 = halved(w3)
    r1, r2, r3, r4 = (rows + 2, rows // 2 + 2, rows // 4 + 2, rows // 8 + 2)
    shapes = (
        (hours, r1, nv, w1),
        (hours, r1, c1, w1),
        (hours, r2, c1, w2),
        (hours, r2, c2, w2),
        (hours, r3, c2, w3),
        (hours, r3, c3, w3),
        (hours, r4, c3, w4),
        (hours, r4, c4, w4),
        (hours, r4, c4, w3),
        (hours, r3, c3, w3),
        (hours, r3, c3, w2),
        (hours, r2, c2, w2),
        (hours, r2, c2, w1),
        (2 * LANES, LANES),
        (LANES, 2 * LANES),
    )
    vmem = pl.BlockSpec(memory_space=pltpu.VMEM)
    result = pl.pallas_call(
        functools.partial(kernel, (nty, ntx, tuple(offsets))),
        out_shape=jax.ShapeDtypeStruct((hours, rows, nv, core), jnp.float32),
        in_specs=[vmem] * 10,
        out_specs=vmem,
        scratch_shapes=[pltpu.VMEM(shape, jnp.bfloat16) for shape in shapes]
        + [pltpu.SemaphoreType.DMA((26,)), pltpu.SemaphoreType.DMA((26,))],
        compiler_params=pltpu.CompilerParams(
            collective_id=0, has_side_effects=True, vmem_limit_bytes=56 * 2**20
        ),
    )(jnp.transpose(fields, (0, 2, 1, 3)), *encoders, *decoders, head_kernel.T, bias)
    return jnp.transpose(result, (0, 2, 1, 3))


def solution(mesh):
    return jax.shard_map(
        functools.partial(body, mesh.shape["ty"], mesh.shape["tx"]),
        mesh=mesh,
        in_specs=(P(None, None, "ty", "tx"),) + (P(),) * 16,
        out_specs=P(None, None, "ty", "tx"),
        check_vma=False,
    )
```

time: 434 us -> 132 us (0.30)
  the two profiles are of different devices: /device:TPU:11 before, /device:TPU:16 now
where the time goes in v1:
time: 132 us
  Pallas kernels  109 us (83%)
  local copies, waits for them, and re-layouts  20.6 us (16%)
  other arithmetic  2.48 us (2%)
    pallas_call x1, Pallas kernels, body(): pl.pallas_call(functools.partial(kernel, (nty, ntx, tuple(offsets))), out...  109 us
    transpose x15, local copies, waits for them, and re-layouts, stacked(): block = jnp.transpose(weights[:, :, start:stop], (1, 3, 0, 2))  5.77 us
    transpose x1, local copies, waits for them, and re-layouts, body(): return jnp.transpose(result, (0, 2, 1, 3))  5.38 us
    unnamed x16, local copies, waits for them, and re-layouts  4.5 us
    reshape x8, local copies, waits for them, and re-layouts, stacked(): blocks.append(block.reshape(3 * weights.shape[3], 3 * (stop - start)))  3.17 us

profile of v1, /device:TPU:16, one launch (start us, length us, event | category | flops | bytes accessed | tf_op | source)
XLA Modules:
  0.0 131.8 jit_solution(12048280130898066014)
XLA Ops:
  0.0 0.0 copy-start.3
  0.0 0.9 concatenate.15
  0.9 1.4 %copy.42 = bf16[32,48]{0,1:T(8,128)(2,1)} copy(bf16[32,48]{1,0:T(8,128)(2,1)} %param.32) | data formatting | bytes 6144 | tf_op args[15]
  2.3 1.0 slice_bitcast_fusion.4
  3.2 0.1 copy.41
  3.3 0.1 reshape.42
  3.4 0.9 slice_bitcast_fusion.5
  4.3 0.0 copy-start.1
  4.3 0.1 copy.40
  4.4 0.1 reshape.41
  4.5 0.7 pad_maximum_fusion.2.d1
  5.2 0.9 copy.32
  6.2 0.7 reshape.33.k1
  6.9 0.9 copy.33
  7.8 0.1 reshape.34
  8.0 0.7 copy.43.k2
  8.7 0.0 copy-done.3
  8.7 0.1 copy.39
  8.9 0.2 reshape.40
  9.1 0.0 copy-start.4
  9.1 0.1 copy.38
  9.2 0.8 pad_maximum_fusion.1.d2
  10.0 0.0 copy-done.1
  10.0 0.2 copy.37
  10.3 0.9 reshape.45.bias
  11.3 0.0 copy-done.4
  11.3 0.3 copy.47
  11.5 0.9 reshape.44.k3
  12.5 0.7 copy.36
  13.2 0.0 copy-start.2
  13.2 0.1 copy.50
  13.3 1.0 pad_maximum_fusion.d3
  14.3 0.0 copy-done.2
  14.3 0.0 copy-start
  14.3 0.6 copy.35
  15.0 0.9 copy.58
  15.9 0.0 copy-done
  15.9 2.0 %copy.57 = bf16[2,48,8,1024]{3,1,2,0:T(8,128)(2,1)} copy(bf16[2,48,8,1024]{3,2,1,0:T(8,128)(2,1)S(1)} %copy-done) | data formatting | bytes 3145728 | tf_op args[0]
  17.9 108.5 %shard_map.163 = f32[2,8,48,1024]{3,2,1,0:T(8,128)} custom-call(bf16[2,8,48,1024]{3,2,1,0:T(8,128)(2,1)} %bitcast.42, bf16[96,144]{1,0:T(8,128)(2,1)} %reshape.33.k1, bf16[192,96]{1,0:T(8,128)(2,1)} %copy.43.k2, bf16[384,192]{1,0:T(8,128)(2,1)} %reshape.44.k3, bf16[768,384]{1,0:T(8,128)(2,1)} %bitcast.46, bf16[384,1152]{1,0:T(8,128)(2,1)} %pad_maximum_fusion.d3, ...), custom_call_target="tpu_custom_call" | custom-call | tf_op jit(solution)/shard_map/pallas_call | solution.py:377
  126.4 5.4 %copy.46 = f32[2,48,8,1024]{3,2,1,0:T(8,128)} copy(f32[2,48,8,1024]{3,1,2,0:T(8,128)} %bitcast.41) | data formatting | bytes 6291456 | tf_op jit(solution)/shard_map/transpose | solution.py:388
  (6 shorter events, 0.2 us)
Async XLA Ops:
  0.0 8.7 %copy-start.3 = (bf16[3,3,192,64]{2,3,1,0:T(8,128)(2,1)S(1)}, bf16[3,3,192,64]{2,3,1,0:T(8,128)(2,1)}, u32[]{:S(2)}) copy-start(bf16[3,3,192,64]{2,3,1,0:T(8,128)(2,1)} %param.28) | copy-start | bytes 663556
  4.3 5.7 %copy-start.1 = (bf16[3,3,384,128]{3,2,1,0:T(8,128)(2,1)S(1)}, bf16[3,3,384,128]{3,2,1,0:T(8,128)(2,1)}, u32[]{:S(2)}) copy-start(bf16[3,3,384,128]{3,2,1,0:T(8,128)(2,1)} %param.26) | copy-start | bytes 2654212
  9.1 2.2 %copy-start.4 = (bf16[3,3,64,128]{3,2,1,0:T(8,128)(2,1)S(1)}, bf16[3,3,64,128]{3,2,1,0:T(8,128)(2,1)}, u32[]{:S(2)}) copy-start(bf16[3,3,64,128]{3,2,1,0:T(8,128)(2,1)} %param.22) | copy-start | bytes 442372
  13.2 1.1 copy-start.2
  14.3 1.6 %copy-start = (bf16[2,48,8,1024]{3,2,1,0:T(8,128)(2,1)S(1)}, bf16[2,48,8,1024]{3,2,1,0:T(8,128)(2,1)}, u32[]{:S(2)}) copy-start(bf16[2,48,8,1024]{3,2,1,0:T(8,128)(2,1)} %param.17) | copy-start | bytes 4718596

commit v2 on v1

v2 whole, which is shorter than its diff:
```python
import functools

import jax
import jax.numpy as jnp
from jax import lax
from jax.experimental import pallas as pl
from jax.experimental.pallas import tpu as pltpu
from jax.sharding import PartitionSpec as P

LANES = 128
MESH = pl.DeviceIdType.MESH


def halved(width):
    return -(-width // (2 * LANES)) * LANES


def kernel(
    sizes,
    fields,
    k1,
    o1,
    k2,
    o2,
    k3,
    o3,
    kc,
    oc,
    d3,
    e3,
    d2,
    e2,
    d1,
    e1,
    hk,
    he,
    out,
    f0,
    s1,
    p1,
    s2,
    p2,
    s3,
    p3,
    c4,
    u3,
    b3,
    u2,
    b2,
    u1,
    pool_m,
    up_m,
    w1,
    w2,
    w3,
    wc,
    x3,
    x2,
    x1,
    wh,
    v1,
    v2,
    v3,
    vc,
    y3,
    y2,
    y1,
    yh,
    send,
    recv,
):
    nty, ntx = sizes
    hours, rows, _, core = fields.shape
    ty, tx = lax.axis_index("ty"), lax.axis_index("tx")
    has_up, has_down = ty > 0, ty < nty - 1
    has_left, has_right = tx > 0, tx < ntx - 1
    far = LANES + core

    for buf in (f0, s1, p1, s2, p2, s3, p3, c4, b3, b2):
        edge = jnp.zeros((buf.shape[0],) + buf.shape[2:], buf.dtype)
        buf[:, 0] = edge
        buf[:, buf.shape[1] - 1] = edge
    side = jnp.zeros((hours, rows) + (f0.shape[2], LANES), f0.dtype)
    f0[:, 1 : rows + 1, :, 0:LANES] = side
    f0[:, 1 : rows + 1, :, far : far + LANES] = side

    barrier = pltpu.get_barrier_semaphore()
    sides = (
        (has_up, {"ty": ty - 1}),
        (has_down, {"ty": ty + 1}),
        (has_left, {"tx": tx - 1}),
        (has_right, {"tx": tx + 1}),
    )
    count = jnp.int32(0)
    for has, where in sides:
        count = count + jnp.where(has, 1, 0)

        @pl.when(has)
        def _():
            pl.semaphore_signal(barrier, inc=1, device_id=where, device_id_type=MESH)

    pl.semaphore_wait(barrier, count)

    def pair(slot, first, second):
        made = []
        for at, (has, other, where, src, dst) in enumerate((first, second)):
            copy = pltpu.make_async_remote_copy(
                src_ref=src,
                dst_ref=dst,
                send_sem=send.at[slot * 2 + at],
                recv_sem=recv.at[slot * 2 + at],
                device_id=where,
                device_id_type=MESH,
            )
            made.append((has, other, copy))

            @pl.when(has)
            def _():
                copy.start()

        def wait():
            for has, other, copy in made:

                @pl.when(has)
                def _():
                    copy.wait_send()

                @pl.when(other)
                def _():
                    copy.wait_recv()

        return wait

    def vertical(slot, top, bottom, after, before):
        return pair(
            slot,
            (has_up, has_down, {"ty": ty - 1}, top, after),
            (has_down, has_up, {"ty": ty + 1}, bottom, before),
        )

    def row_exchange(slot, buf):
        last = buf.shape[1] - 1
        return vertical(slot, buf.at[:, 1], buf.at[:, last - 1], buf.at[:, last], buf.at[:, 0])

    middle = pl.ds(LANES, core)
    wait_sides = pair(
        0,
        (
            has_left,
            has_right,
            {"tx": tx - 1},
            fields.at[:, :, :, pl.ds(0, LANES)],
            f0.at[:, pl.ds(1, rows), :, pl.ds(far, LANES)],
        ),
        (
            has_right,
            has_left,
            {"tx": tx + 1},
            fields.at[:, :, :, pl.ds(core - LANES, LANES)],
            f0.at[:, pl.ds(1, rows), :, pl.ds(0, LANES)],
        ),
    )
    wait_rows = vertical(
        1,
        fields.at[:, 0],
        fields.at[:, rows - 1],
        f0.at[:, rows + 1, :, middle],
        f0.at[:, 0, :, middle],
    )

    f0[:, 1 : rows + 1, :, LANES:far] = fields[...]
    two, one = 2 * LANES, LANES
    tall = lax.broadcasted_iota(jnp.int32, (two, one), 0)
    wide = lax.broadcasted_iota(jnp.int32, (two, one), 1)
    pool_m[...] = jnp.where(lax.shift_right_logical(tall, 1) == wide, 0.25, 0.0).astype(jnp.bfloat16)
    tall = lax.broadcasted_iota(jnp.int32, (one, two), 0)
    wide = lax.broadcasted_iota(jnp.int32, (one, two), 1)
    up_m[...] = jnp.where(lax.shift_right_logical(wide, 1) == tall, 1.0, 0.0).astype(jnp.bfloat16)

    def eye(n):
        down = lax.broadcasted_iota(jnp.int32, (n, n), 0)
        across = lax.broadcasted_iota(jnp.int32, (n, n), 1)
        return down == across

    def turned(block):
        return lax.dot_general(
            jnp.where(eye(block.shape[1]), 1.0, 0.0).astype(jnp.bfloat16),
            block,
            (((1,), (1,)), ((), ())),
            preferred_element_type=jnp.float32,
        ).astype(jnp.bfloat16)

    def arrange(src, dst, cuts):
        size = src.shape[3]
        count = dst.shape[0] // (3 * size)
        for off in range(count):
            for c in range(3):
                blocks = []
                for start, stop in cuts:
                    zero = jnp.zeros((stop - start, size), jnp.bfloat16)
                    taken = src[:, c, start:stop].reshape(3 * (stop - start), size)
                    blocks += [zero] * off + [taken] + [zero] * (count - 1 - off)
                block = blocks[0] if len(blocks) == 1 else jnp.concatenate(blocks, axis=0)
                at = (off * 3 + c) * size
                dst[at : at + size] = turned(block)

    def upright(src, dst):
        n = src.shape[0]
        row = jnp.broadcast_to(src[...].reshape(1, n), (n, n))
        dst[...] = jnp.sum(jnp.where(eye(n), row, 0.0), axis=1, keepdims=True)

    for src, dst in ((k1, w1), (k2, w2), (k3, w3), (kc, wc)):
        arrange(src, dst, ((0, src.shape[2]),))
    for src, dst, low in ((d3, x3, c4), (d2, x2, b3), (d1, x1, b2)):
        arrange(src, dst, ((0, low.shape[2]), (low.shape[2], src.shape[2])))
    wh[...] = turned(hk[...])
    for src, dst in zip((o1, o2, o3, oc, e3, e2, e1, he), (v1, v2, v3, vc, y3, y2, y1, yh)):
        upright(src, dst)

    wait_sides()
    waits = []
    for at, start in enumerate((0, far)):
        lanes = pl.ds(start, LANES)
        waits.append(
            vertical(
                2 + at,
                f0.at[:, 1, :, lanes],
                f0.at[:, rows, :, lanes],
                f0.at[:, rows + 1, :, lanes],
                f0.at[:, 0, :, lanes],
            )
        )
    wait_rows()
    for wait in waits:
        wait()

    def inside(width, level):
        column = lax.broadcasted_iota(jnp.int32, (1, width), 1)
        column = column + (tx * (core >> level) - (LANES >> level))
        return (column >= 0) & (column < ntx * (core >> level))

    def conv(weights, offset, operand, level):
        width = operand.shape[1]
        size = offset.shape[0]
        terms = jnp.dot(weights[...], operand, preferred_element_type=jnp.float32)
        made = []
        for at in range(0, terms.shape[0], 3 * size):
            total = terms[at + size : at + 2 * size] + offset[...]
            total = total + pltpu.roll(terms[at : at + size], 1, 1)
            total = total + pltpu.roll(terms[at + 2 * size : at + 3 * size], width - 1, 1)
            half = 0.5 * total
            result = half * jnp.tanh(half) + half
            if level is not None:
                result = jnp.where(inside(width, level), result, 0.0)
            made.append(result.astype(jnp.bfloat16))
        return made

    def pooled(values):
        width = values[0].shape[1]
        size = values[0].shape[0]
        tall = jnp.concatenate(values, axis=0)
        pieces = []
        for start in range(0, width, two):
            stop = min(start + two, width)
            pieces.append(
                jnp.dot(tall[:, start:stop], pool_m[0 : stop - start], preferred_element_type=jnp.float32)
            )
        sums = jnp.concatenate(pieces, axis=1)
        return [
            (sums[at : at + size] + sums[at + size : at + 2 * size]).astype(jnp.bfloat16)
            for at in range(0, size * len(values), 2 * size)
        ]

    def widen(src, dst, first, last):
        width = dst.shape[3]
        size = src.shape[2]
        n = last - first
        for start in range(0, width, two):
            stop = min(start + two, width)
            block = src[:, first:last, :, start // 2 : start // 2 + one]
            wide = jnp.dot(
                block.reshape(hours * n * size, one),
                up_m[:, 0 : stop - start],
                preferred_element_type=jnp.float32,
            ).astype(jnp.bfloat16)
            dst[:, first:last, :, start:stop] = wide.reshape(hours, n, size, stop - start)

    def taps(buf, h, r, n):
        block = buf[h, pl.ds(r, n)]
        return block.reshape(n * buf.shape[2], buf.shape[3])

    def edges(half, step):
        if half == 1:
            step(0)
            return

        def both(j, carry):
            step(j * (half - 1))
            return carry

        lax.fori_loop(0, 2, both, 0)

    def interior(half, step):
        def one_pair(j, carry):
            step(j)
            return carry

        if half > 2:
            lax.fori_loop(1, half - 1, one_pair, 0)

    def encode(src, weights, offset, dst, nxt, level, slot):
        half = (src.shape[1] - 2) // 2

        def step(i):
            made = []
            for h in range(hours):
                pair_of = conv(weights, offset, taps(src, h, 2 * i, 4), level)
                for off, row in enumerate(pair_of):
                    dst[h, 2 * i + off + 1] = row
                made += pair_of
            for h, row in enumerate(pooled(made)):
                nxt[h, i + 1] = row

        edges(half, step)
        waits = row_exchange(slot, nxt), row_exchange(slot + 1, dst)
        interior(half, step)
        return waits

    def decode(low, up, skip, weights, offset, write, level, wait):
        half = (skip.shape[1] - 2) // 2
        last = low.shape[1] - 1

        def step(i):
            for h in range(hours):
                above, here, below = up[h, i], up[h, i + 1], up[h, i + 2]
                operand = jnp.concatenate(
                    (above, here, here, below, taps(skip, h, 2 * i, 4)), axis=0
                )
                for off, row in enumerate(conv(weights, offset, operand, level)):
                    write(h, 2 * i + off, row)

        widen(low, up, 1, last)
        interior(half, step)
        wait()
        widen(low, up, 0, 1)
        widen(low, up, last, last + 1)
        edges(half, step)

    wait_p1, wait_s1 = encode(f0, w1, v1, s1, p1, 0, 4)
    wait_p1()
    wait_p2, wait_s2 = encode(p1, w2, v2, s2, p2, 1, 6)
    wait_p2()
    wait_p3, wait_s3 = encode(p2, w3, v3, s3, p3, 2, 8)
    wait_p3()
    for h in range(hours):
        for r in range(c4.shape[1] - 2):
            (c4[h, r + 1],) = conv(wc, vc, taps(p3, h, r, 3), 3)
    wait_c4 = row_exchange(10, c4)
    wait_s3()

    def keep(buf):
        def write(h, r, value):
            buf[h, r + 1] = value

        return write

    decode(c4, u3, s3, x3, y3, keep(b3), 2, wait_c4)
    wait_b3 = row_exchange(11, b3)
    wait_s2()
    decode(b3, u2, s2, x2, y2, keep(b2), 1, wait_b3)
    wait_b2 = row_exchange(12, b2)
    wait_s1()

    def head(h, r, value):
        total = jnp.dot(wh[...], value[:, LANES:far], preferred_element_type=jnp.float32)
        total = total + yh[...]
        out[h, r] = total + f0[h, r + 1, :, LANES:far].astype(jnp.float32)

    decode(b2, u1, s1, x1, y1, head, None, wait_b2)


def body(nty, ntx, fields, *weights):
    hours, nv, rows, core = fields.shape
    sizes = [k.shape[3] for k in weights[0:8:2]]
    c1, c2, c3, c4 = sizes
    w1 = core + 2 * LANES
    w2 = halved(w1)
    w3 = halved(w2)
    w4 = halved(w3)
    r1, r2, r3, r4 = (rows + 2, rows // 2 + 2, rows // 4 + 2, rows // 8 + 2)
    shapes = (
        (hours, r1, nv, w1),
        (hours, r1, c1, w1),
        (hours, r2, c1, w2),
        (hours, r2, c2, w2),
        (hours, r3, c2, w3),
        (hours, r3, c3, w3),
        (hours, r4, c3, w4),
        (hours, r4, c4, w4),
        (hours, r4, c4, w3),
        (hours, r3, c3, w3),
        (hours, r3, c3, w2),
        (hours, r2, c2, w2),
        (hours, r2, c2, w1),
        (2 * LANES, LANES),
        (LANES, 2 * LANES),
        (6 * c1, 4 * nv),
        (6 * c2, 4 * c1),
        (6 * c3, 4 * c2),
        (3 * c4, 3 * c3),
        (6 * c3, 4 * (c4 + c3)),
        (6 * c2, 4 * (c3 + c2)),
        (6 * c1, 4 * (c2 + c1)),
        (nv, c1),
    )
    columns = (c1, c2, c3, c4, c3, c2, c1, nv)
    vmem = pl.BlockSpec(memory_space=pltpu.VMEM)
    result = pl.pallas_call(
        functools.partial(kernel, (nty, ntx)),
        out_shape=jax.ShapeDtypeStruct((hours, rows, nv, core), jnp.float32),
        in_specs=[vmem] * 17,
        out_specs=vmem,
        scratch_shapes=[pltpu.VMEM(shape, jnp.bfloat16) for shape in shapes]
        + [pltpu.VMEM((n, 1), jnp.float32) for n in columns]
        + [pltpu.SemaphoreType.DMA((26,)), pltpu.SemaphoreType.DMA((26,))],
        compiler_params=pltpu.CompilerParams(
            collective_id=0, has_side_effects=True, vmem_limit_bytes=56 * 2**20
        ),
    )(jnp.transpose(fields, (0, 2, 1, 3)), *weights)
    return jnp.transpose(result, (0, 2, 1, 3))


def solution(mesh):
    return jax.shard_map(
        functools.partial(body, mesh.shape["ty"], mesh.shape["tx"]),
        mesh=mesh,
        in_specs=(P(None, None, "ty", "tx"),) + (P(),) * 16,
        out_specs=P(None, None, "ty", "tx"),
        check_vma=False,
    )
```

time: 132 us -> 110 us (0.83)
  Pallas kernels: 109 us -> 95.8 us
  local copies, waits for them, and re-layouts: 20.6 us -> 14 us
  other arithmetic: 2.48 us -> 0 us
    pallas_call x1, Pallas kernels: 109 us -> 95.8 us  [body(): pl.pallas_call(functools.partial(kernel, (nty, ntx)), out_shape=jax.Shape...]
    transpose x15 -> x0, local copies, waits for them, and re-layouts: 5.77 us -> none  [stacked(): block = jnp.transpose(weights[:, :, start:stop], (1, 3, 0, 2))]
    unnamed x16 -> x4, local copies, waits for them, and re-layouts: 4.5 us -> 8.67 us
    reshape x9 -> x0, local copies, waits for them, and re-layouts: 4.1 us -> none  [the longest x8 3.17 us: stacked(): blocks.append(block.reshape(3 * weights.shape[3], 3 * (stop - start)))]
    concatenate x3 -> x0, other arithmetic: 2.48 us -> none  [stacked(): return blocks[0] if len(blocks) == 1 else jnp.concatenate(blocks, axis=1)]
where the time goes in v2:
time: 110 us
  Pallas kernels  95.8 us (87%)
  local copies, waits for them, and re-layouts  14 us (13%)
    pallas_call x1, Pallas kernels, body(): pl.pallas_call(functools.partial(kernel, (nty, ntx)), out_shape=jax.Shape...  95.8 us
    unnamed x4, local copies, waits for them, and re-layouts  8.67 us
    transpose x1, local copies, waits for them, and re-layouts, body(): return jnp.transpose(result, (0, 2, 1, 3))  5.38 us

profile of v2, /device:TPU:16, one launch (start us, length us, event | category | flops | bytes accessed | tf_op | source)
XLA Modules:
  0.0 109.9 jit_solution(7254448681965553149)
XLA Ops:
  0.0 1.6 %copy.19.k1 = bf16[3,3,48,32]{3,2,1,0:T(8,128)(2,1)} copy(bf16[3,3,48,32]{2,3,1,0:T(8,128)(2,1)} %param.18) | data formatting | bytes 55296 | tf_op args[1]
  1.6 1.7 %copy.21.d1 = bf16[3,3,96,32]{3,2,1,0:T(8,128)(2,1)} copy(bf16[3,3,96,32]{2,3,1,0:T(8,128)(2,1)} %param.30) | data formatting | bytes 110592 | tf_op args[13]
  3.3 1.9 %copy.20.d2 = bf16[3,3,192,64]{3,2,1,0:T(8,128)(2,1)} copy(bf16[3,3,192,64]{2,3,1,0:T(8,128)(2,1)} %param.28) | data formatting | bytes 442368 | tf_op args[11]
  5.3 3.4 %copy.24 = bf16[2,48,8,1024]{3,1,2,0:T(8,128)(2,1)} copy(bf16[2,48,8,1024]{3,2,1,0:T(8,128)(2,1)} %param.17) | data formatting | bytes 3145728 | tf_op args[0]
  8.7 95.8 %shard_map.163 = f32[2,8,48,1024]{3,2,1,0:T(8,128)} custom-call(bf16[2,8,48,1024]{3,2,1,0:T(8,128)(2,1)} %bitcast.5, bf16[3,3,48,32]{3,2,1,0:T(8,128)(2,1)} %copy.19.k1, f32[32]{0:T(128)} %o1.1, bf16[3,3,32,64]{3,2,1,0:T(8,128)(2,1)} %k2.1, f32[64]{0:T(128)} %o2.1, bf16[3,3,64,128]{3,2,1,0:T(8,128)(2,1)} %k3.1, f32[128]{0:T(128)} %o3.1, ...), custom_call_target="tpu_custom_call" | custom-call | tf_op jit(solution)/shard_map/pallas_call | solution.py:418
  104.5 5.4 %copy.22 = f32[2,48,8,1024]{3,2,1,0:T(8,128)} copy(f32[2,48,8,1024]{3,1,2,0:T(8,128)} %bitcast.4) | data formatting | bytes 6291456 | tf_op jit(solution)/shard_map/transpose | solution.py:430

commit v3 on v2

--- a/solution.py
+++ b/solution.py
@@ -66,6 +66,12 @@
     y2,
     y1,
     yh,
+    q3,
+    g3,
+    q2,
+    g2,
+    q1,
+    g1,
     send,
     recv,
 ):
@@ -76,10 +82,12 @@
     has_left, has_right = tx > 0, tx < ntx - 1
     far = LANES + core
 
-    for buf in (f0, s1, p1, s2, p2, s3, p3, c4, b3, b2):
+    for buf in (f0, s1, p1, s2, p2, s3, p3, u3, u2, u1):
         edge = jnp.zeros((buf.shape[0],) + buf.shape[2:], buf.dtype)
         buf[:, 0] = edge
         buf[:, buf.shape[1] - 1] = edge
+    for buf in (g3, g2, g1):
+        buf[...] = jnp.zeros(buf.shape, buf.dtype)
     side = jnp.zeros((hours, rows) + (f0.shape[2], LANES), f0.dtype)
     f0[:, 1 : rows + 1, :, 0:LANES] = side
     f0[:, 1 : rows + 1, :, far : far + LANES] = side
@@ -191,14 +199,19 @@
         ).astype(jnp.bfloat16)
 
     def arrange(src, dst, cuts):
-        size = src.shape[3]
+        straight = src.shape[2] == cuts[-1][1]
+        size = src.shape[3] if straight else src.shape[2]
         count = dst.shape[0] // (3 * size)
-        for off in range(count):
-            for c in range(3):
+        for c in range(3):
+            if straight:
+                rows_of = src[:, c]
+            else:
+                rows_of = jnp.stack([turned(src[a, c]) for a in range(3)])
+            for off in range(count):
                 blocks = []
                 for start, stop in cuts:
                     zero = jnp.zeros((stop - start, size), jnp.bfloat16)
-                    taken = src[:, c, start:stop].reshape(3 * (stop - start), size)
+                    taken = rows_of[:, start:stop].reshape(3 * (stop - start), size)
                     blocks += [zero] * off + [taken] + [zero] * (count - 1 - off)
                 block = blocks[0] if len(blocks) == 1 else jnp.concatenate(blocks, axis=0)
                 at = (off * 3 + c) * size
@@ -209,10 +222,11 @@
         row = jnp.broadcast_to(src[...].reshape(1, n), (n, n))
         dst[...] = jnp.sum(jnp.where(eye(n), row, 0.0), axis=1, keepdims=True)
 
-    for src, dst in ((k1, w1), (k2, w2), (k3, w3), (kc, wc)):
-        arrange(src, dst, ((0, src.shape[2]),))
-    for src, dst, low in ((d3, x3, c4), (d2, x2, b3), (d1, x1, b2)):
-        arrange(src, dst, ((0, low.shape[2]), (low.shape[2], src.shape[2])))
+    for src, dst, buf in ((k1, w1, f0), (k2, w2, p1), (k3, w3, p2), (kc, wc, p3)):
+        arrange(src, dst, ((0, buf.shape[2]),))
+    for src, dst, low, skip in ((d3, x3, c4, s3), (d2, x2, b3, s2), (d1, x1, b2, s1)):
+        cut = low.shape[2]
+        arrange(src, dst, ((0, cut), (cut, cut + skip.shape[2])))
     wh[...] = turned(hk[...])
     for src, dst in zip((o1, o2, o3, oc, e3, e2, e1, he), (v1, v2, v3, vc, y3, y2, y1, yh)):
         upright(src, dst)
@@ -239,19 +253,27 @@
         column = column + (tx * (core >> level) - (LANES >> level))
         return (column >= 0) & (column < ntx * (core >> level))
 
-    def conv(weights, offset, operand, level):
+    def combined(weights, size, operand, lanes):
         width = operand.shape[1]
-        size = offset.shape[0]
         terms = jnp.dot(weights[...], operand, preferred_element_type=jnp.float32)
         made = []
         for at in range(0, terms.shape[0], 3 * size):
-            total = terms[at + size : at + 2 * size] + offset[...]
+            total = terms[at + size : at + 2 * size]
             total = total + pltpu.roll(terms[at : at + size], 1, 1)
             total = total + pltpu.roll(terms[at + 2 * size : at + 3 * size], width - 1, 1)
+            made.append(total if lanes is None else total[:, lanes[0] : lanes[1]])
+        return made
+
+    def conv(weights, offset, operand, level, lanes=None, more=(None, None)):
+        made = []
+        for total, extra in zip(combined(weights, offset.shape[0], operand, lanes), more):
+            total = total + offset[...]
+            if extra is not None:
+                total = total + extra.astype(jnp.float32)
             half = 0.5 * total
             result = half * jnp.tanh(half) + half
             if level is not None:
-                result = jnp.where(inside(width, level), result, 0.0)
+                result = jnp.where(inside(result.shape[1], level), result, 0.0)
             made.append(result.astype(jnp.bfloat16))
         return made
 
@@ -322,41 +344,51 @@
                 nxt[h, i + 1] = row
 
         edges(half, step)
-        waits = row_exchange(slot, nxt), row_exchange(slot + 1, dst)
+        wait = row_exchange(slot, nxt)
         interior(half, step)
-        return waits
-
-    def decode(low, up, skip, weights, offset, write, level, wait):
+        return wait
+
+    def decode(low, up, skip, weights, offset, write, level, slot, sums, given):
         half = (skip.shape[1] - 2) // 2
-        last = low.shape[1] - 1
-
-        def step(i):
+        last, end = low.shape[1] - 2, skip.shape[1] - 2
+        lanes = (LANES, far) if level is None else None
+
+        def step(i, top=False, bottom=False):
             for h in range(hours):
                 above, here, below = up[h, i], up[h, i + 1], up[h, i + 2]
                 operand = jnp.concatenate(
                     (above, here, here, below, taps(skip, h, 2 * i, 4)), axis=0
                 )
-                for off, row in enumerate(conv(weights, offset, operand, level)):
+                more = (given[0, h] if top else None, given[1, h] if bottom else None)
+                made = conv(weights, offset, operand, level, lanes, more)
+                for off, row in enumerate(made):
                     write(h, 2 * i + off, row)
 
-        widen(low, up, 1, last)
+        widen(low, up, 1, last + 1)
+        for h in range(hours):
+            blank, empty = jnp.zeros_like(up[h, 1]), jnp.zeros_like(skip[h, 1])
+            operand = jnp.concatenate(
+                (up[h, last], blank, blank, up[h, 1])
+                + (skip[h, end], empty, empty, skip[h, 1]),
+                axis=0,
+            )
+            for at, total in enumerate(combined(weights, offset.shape[0], operand, lanes)):
+                sums[at, h] = total.astype(jnp.bfloat16)
+        wait = vertical(slot, sums.at[1], sums.at[0], given.at[1], given.at[0])
         interior(half, step)
         wait()
-        widen(low, up, 0, 1)
-        widen(low, up, last, last + 1)
-        edges(half, step)
-
-    wait_p1, wait_s1 = encode(f0, w1, v1, s1, p1, 0, 4)
-    wait_p1()
-    wait_p2, wait_s2 = encode(p1, w2, v2, s2, p2, 1, 6)
-    wait_p2()
-    wait_p3, wait_s3 = encode(p2, w3, v3, s3, p3, 2, 8)
-    wait_p3()
+        if half == 1:
+            step(0, True, True)
+        else:
+            step(0, True, False)
+            step(half - 1, False, True)
+
+    encode(f0, w1, v1, s1, p1, 0, 4)()
+    encode(p1, w2, v2, s2, p2, 1, 5)()
+    encode(p2, w3, v3, s3, p3, 2, 6)()
     for h in range(hours):
         for r in range(c4.shape[1] - 2):
             (c4[h, r + 1],) = conv(wc, vc, taps(p3, h, r, 3), 3)
-    wait_c4 = row_exchange(10, c4)
-    wait_s3()
 
     def keep(buf):
         def write(h, r, value):
@@ -364,19 +396,19 @@
 
         return write
 
-    decode(c4, u3, s3, x3, y3, keep(b3), 2, wait_c4)
-    wait_b3 = row_exchange(11, b3)
-    wait_s2()
-    decode(b3, u2, s2, x2, y2, keep(b2), 1, wait_b3)
-    wait_b2 = row_exchange(12, b2)
-    wait_s1()
+    decode(c4, u3, s3, x3, y3, keep(b3), 2, 7, q3, g3)
+    decode(b3, u2, s2, x2, y2, keep(b2), 1, 8, q2, g2)
 
     def head(h, r, value):
-        total = jnp.dot(wh[...], value[:, LANES:far], preferred_element_type=jnp.float32)
+        total = jnp.dot(wh[...], value, preferred_element_type=jnp.float32)
         total = total + yh[...]
         out[h, r] = total + f0[h, r + 1, :, LANES:far].astype(jnp.float32)
 
-    decode(b2, u1, s1, x1, y1, head, None, wait_b2)
+    decode(b2, u1, s1, x1, y1, head, None, 9, q1, g1)
+
+
+def narrow(depth, size):
+    return size < LANES and size < depth
 
 
 def body(nty, ntx, fields, *weights):
@@ -413,6 +445,15 @@
         (6 * c1, 4 * (c2 + c1)),
         (nv, c1),
     )
+    swapped = [
+        jnp.swapaxes(k, 2, 3) if k.ndim == 4 and narrow(k.shape[2], k.shape[3]) else k
+        for k in weights
+    ]
+    sums = [
+        (2, hours, n, width)
+        for n, width in ((c3, w3), (c2, w2), (c1, core))
+        for _ in range(2)
+    ]
     columns = (c1, c2, c3, c4, c3, c2, c1, nv)
     vmem = pl.BlockSpec(memory_space=pltpu.VMEM)
     result = pl.pallas_call(
@@ -422,11 +463,12 @@
         out_specs=vmem,
         scratch_shapes=[pltpu.VMEM(shape, jnp.bfloat16) for shape in shapes]
         + [pltpu.VMEM((n, 1), jnp.float32) for n in columns]
-        + [pltpu.SemaphoreType.DMA((26,)), pltpu.SemaphoreType.DMA((26,))],
+        + [pltpu.VMEM(shape, jnp.bfloat16) for shape in sums]
+        + [pltpu.SemaphoreType.DMA((20,)), pltpu.SemaphoreType.DMA((20,))],
         compiler_params=pltpu.CompilerParams(
             collective_id=0, has_side_effects=True, vmem_limit_bytes=56 * 2**20
         ),
-    )(jnp.transpose(fields, (0, 2, 1, 3)), *weights)
+    )(jnp.transpose(fields, (0, 2, 1, 3)), *swapped)
     return jnp.transpose(result, (0, 2, 1, 3))
 
 

time: 110 us -> 85.4 us (0.78)
  Pallas kernels: 95.8 us -> 76.4 us
  local copies, waits for them, and re-layouts: 14 us -> 8.79 us
    pallas_call x1, Pallas kernels: 95.8 us -> 76.4 us  [body(): pl.pallas_call(functools.partial(kernel, (nty, ntx)), out_shape=jax.Shape...]
    unnamed x4 -> x1, local copies, waits for them, and re-layouts: 8.67 us -> 3.41 us
where the time goes in v3:
time: 85.4 us; the launch traced here: 85.2 us
  Pallas kernels  76.4 us (89%)
  local copies, waits for them, and re-layouts  8.79 us (10%)
    pallas_call x1, Pallas kernels, body(): pl.pallas_call(functools.partial(kernel, (nty, ntx)), out_shape=jax.Shape...  76.4 us
    transpose x1, local copies, waits for them, and re-layouts, body(): return jnp.transpose(result, (0, 2, 1, 3))  5.38 us
    unnamed x1, local copies, waits for them, and re-layouts  3.41 us

profile of v3, /device:TPU:16, one launch (start us, length us, event | category | flops | bytes accessed | tf_op | source)
XLA Modules:
  0.0 85.2 jit_solution(17997474745763340400)
XLA Ops:
  0.0 3.4 %copy.21 = bf16[2,48,8,1024]{3,1,2,0:T(8,128)(2,1)} copy(bf16[2,48,8,1024]{3,2,1,0:T(8,128)(2,1)} %param.17) | data formatting | bytes 3145728 | tf_op args[0]
  3.4 76.4 %shard_map.163 = f32[2,8,48,1024]{3,2,1,0:T(8,128)} custom-call(bf16[2,8,48,1024]{3,2,1,0:T(8,128)(2,1)} %bitcast.8, bf16[3,3,32,48]{3,2,1,0:T(8,128)(2,1)} %bitcast.10, f32[32]{0:T(128)} %o1.1, bf16[3,3,32,64]{3,2,1,0:T(8,128)(2,1)} %k2.1, f32[64]{0:T(128)} %o2.1, bf16[3,3,64,128]{3,2,1,0:T(8,128)(2,1)} %k3.1, f32[128]{0:T(128)} %o3.1, ...), custom_call_target="tpu_custom_call" | custom-call | tf_op jit(solution)/shard_map/pallas_call | solution.py:459
  79.8 5.4 %copy.19 = f32[2,48,8,1024]{3,2,1,0:T(8,128)} copy(f32[2,48,8,1024]{3,1,2,0:T(8,128)} %bitcast.7) | data formatting | bytes 6291456 | tf_op jit(solution)/shard_map/transpose | solution.py:472

commit v4 on v3

--- a/solution.py
+++ b/solution.py
@@ -109,8 +109,10 @@
 
     pl.semaphore_wait(barrier, count)
 
-    def pair(slot, first, second):
-        made = []
+    slots = iter(range(send.shape[0] // 2))
+
+    def pair(first, second):
+        made, slot = [], next(slots)
         for at, (has, other, where, src, dst) in enumerate((first, second)):
             copy = pltpu.make_async_remote_copy(
                 src_ref=src,
@@ -139,42 +141,45 @@
 
         return wait
 
-    def vertical(slot, top, bottom, after, before):
+    def vertical(top, bottom, after, before):
         return pair(
-            slot,
             (has_up, has_down, {"ty": ty - 1}, top, after),
             (has_down, has_up, {"ty": ty + 1}, bottom, before),
         )
 
-    def row_exchange(slot, buf):
+    def row_exchange(buf, h):
         last = buf.shape[1] - 1
-        return vertical(slot, buf.at[:, 1], buf.at[:, last - 1], buf.at[:, last], buf.at[:, 0])
+        return vertical(buf.at[h, 1], buf.at[h, last - 1], buf.at[h, last], buf.at[h, 0])
+
+    def column_exchange(h):
+        return pair(
+            (
+                has_left,
+                has_right,
+                {"tx": tx - 1},
+                fields.at[h, :, :, pl.ds(0, LANES)],
+                f0.at[h, pl.ds(1, rows), :, pl.ds(far, LANES)],
+            ),
+            (
+                has_right,
+                has_left,
+                {"tx": tx + 1},
+                fields.at[h, :, :, pl.ds(core - LANES, LANES)],
+                f0.at[h, pl.ds(1, rows), :, pl.ds(0, LANES)],
+            ),
+        )
 
     middle = pl.ds(LANES, core)
-    wait_sides = pair(
-        0,
-        (
-            has_left,
-            has_right,
-            {"tx": tx - 1},
-            fields.at[:, :, :, pl.ds(0, LANES)],
-            f0.at[:, pl.ds(1, rows), :, pl.ds(far, LANES)],
-        ),
-        (
-            has_right,
-            has_left,
-            {"tx": tx + 1},
-            fields.at[:, :, :, pl.ds(core - LANES, LANES)],
-            f0.at[:, pl.ds(1, rows), :, pl.ds(0, LANES)],
-        ),
-    )
-    wait_rows = vertical(
-        1,
-        fields.at[:, 0],
-        fields.at[:, rows - 1],
-        f0.at[:, rows + 1, :, middle],
-        f0.at[:, 0, :, middle],
-    )
+    wait_sides = [column_exchange(h) for h in range(hours)]
+    wait_rows = [
+        vertical(
+            fields.at[h, 0],
+            fields.at[h, rows - 1],
+            f0.at[h, rows + 1, :, middle],
+            f0.at[h, 0, :, middle],
+        )
+        for h in range(hours)
+    ]
 
     f0[:, 1 : rows + 1, :, LANES:far] = fields[...]
     two, one = 2 * LANES, LANES
@@ -222,32 +227,6 @@
         row = jnp.broadcast_to(src[...].reshape(1, n), (n, n))
         dst[...] = jnp.sum(jnp.where(eye(n), row, 0.0), axis=1, keepdims=True)
 
-    for src, dst, buf in ((k1, w1, f0), (k2, w2, p1), (k3, w3, p2), (kc, wc, p3)):
-        arrange(src, dst, ((0, buf.shape[2]),))
-    for src, dst, low, skip in ((d3, x3, c4, s3), (d2, x2, b3, s2), (d1, x1, b2, s1)):
-        cut = low.shape[2]
-        arrange(src, dst, ((0, cut), (cut, cut + skip.shape[2])))
-    wh[...] = turned(hk[...])
-    for src, dst in zip((o1, o2, o3, oc, e3, e2, e1, he), (v1, v2, v3, vc, y3, y2, y1, yh)):
-        upright(src, dst)
-
-    wait_sides()
-    waits = []
-    for at, start in enumerate((0, far)):
-        lanes = pl.ds(start, LANES)
-        waits.append(
-            vertical(
-                2 + at,
-                f0.at[:, 1, :, lanes],
-                f0.at[:, rows, :, lanes],
-                f0.at[:, rows + 1, :, lanes],
-                f0.at[:, 0, :, lanes],
-            )
-        )
-    wait_rows()
-    for wait in waits:
-        wait()
-
     def inside(width, level):
         column = lax.broadcasted_iota(jnp.int32, (1, width), 1)
         column = column + (tx * (core >> level) - (LANES >> level))
@@ -293,34 +272,23 @@
             for at in range(0, size * len(values), 2 * size)
         ]
 
-    def widen(src, dst, first, last):
+    def widen(src, dst, h, first, last):
         width = dst.shape[3]
         size = src.shape[2]
         n = last - first
         for start in range(0, width, two):
             stop = min(start + two, width)
-            block = src[:, first:last, :, start // 2 : start // 2 + one]
+            block = src[h, first:last, :, start // 2 : start // 2 + one]
             wide = jnp.dot(
-                block.reshape(hours * n * size, one),
+                block.reshape(n * size, one),
                 up_m[:, 0 : stop - start],
                 preferred_element_type=jnp.float32,
             ).astype(jnp.bfloat16)
-            dst[:, first:last, :, start:stop] = wide.reshape(hours, n, size, stop - start)
+            dst[h, first:last, :, start:stop] = wide.reshape(n, size, stop - start)
 
     def taps(buf, h, r, n):
         block = buf[h, pl.ds(r, n)]
         return block.reshape(n * buf.shape[2], buf.shape[3])
-
-    def edges(half, step):
-        if half == 1:
-            step(0)
-            return
-
-        def both(j, carry):
-            step(j * (half - 1))
-            return carry
-
-        lax.fori_loop(0, 2, both, 0)
 
     def interior(half, step):
         def one_pair(j, carry):
@@ -330,31 +298,32 @@
         if half > 2:
             lax.fori_loop(1, half - 1, one_pair, 0)
 
-    def encode(src, weights, offset, dst, nxt, level, slot):
+    def encoder(src, weights, offset, dst, nxt, level):
         half = (src.shape[1] - 2) // 2
 
-        def step(i):
-            made = []
-            for h in range(hours):
-                pair_of = conv(weights, offset, taps(src, h, 2 * i, 4), level)
-                for off, row in enumerate(pair_of):
+        def inner(h):
+            def step(i):
+                made = conv(weights, offset, taps(src, h, 2 * i, 4), level)
+                for off, row in enumerate(made):
                     dst[h, 2 * i + off + 1] = row
-                made += pair_of
-            for h, row in enumerate(pooled(made)):
-                nxt[h, i + 1] = row
-
-        edges(half, step)
-        wait = row_exchange(slot, nxt)
-        interior(half, step)
-        return wait
-
-    def decode(low, up, skip, weights, offset, write, level, slot, sums, given):
+                (nxt[h, i + 1],) = pooled(made)
+
+            return step
+
+        def outer(h):
+            for i in sorted({0, half - 1}):
+                inner(h)(i)
+            return row_exchange(nxt, h)
+
+        return lambda h: interior(half, inner(h)), outer
+
+    def decoder(low, up, skip, weights, offset, write, level, sums, given):
         half = (skip.shape[1] - 2) // 2
         last, end = low.shape[1] - 2, skip.shape[1] - 2
         lanes = (LANES, far) if level is None else None
 
-        def step(i, top=False, bottom=False):
-            for h in range(hours):
+        def inner(h, top=False, bottom=False):
+            def step(i):
                 above, here, below = up[h, i], up[h, i + 1], up[h, i + 2]
                 operand = jnp.concatenate(
                     (above, here, here, below, taps(skip, h, 2 * i, 4)), axis=0
@@ -364,8 +333,10 @@
                 for off, row in enumerate(made):
                     write(h, 2 * i + off, row)
 
-        widen(low, up, 1, last + 1)
-        for h in range(hours):
+            return step
+
+        def begin(h):
+            widen(low, up, h, 1, last + 1)
             blank, empty = jnp.zeros_like(up[h, 1]), jnp.zeros_like(skip[h, 1])
             operand = jnp.concatenate(
                 (up[h, last], blank, blank, up[h, 1])
@@ -374,37 +345,114 @@
             )
             for at, total in enumerate(combined(weights, offset.shape[0], operand, lanes)):
                 sums[at, h] = total.astype(jnp.bfloat16)
-        wait = vertical(slot, sums.at[1], sums.at[0], given.at[1], given.at[0])
-        interior(half, step)
-        wait()
-        if half == 1:
-            step(0, True, True)
-        else:
-            step(0, True, False)
-            step(half - 1, False, True)
-
-    encode(f0, w1, v1, s1, p1, 0, 4)()
-    encode(p1, w2, v2, s2, p2, 1, 5)()
-    encode(p2, w3, v3, s3, p3, 2, 6)()
-    for h in range(hours):
-        for r in range(c4.shape[1] - 2):
-            (c4[h, r + 1],) = conv(wc, vc, taps(p3, h, r, 3), 3)
+            return vertical(sums.at[1, h], sums.at[0, h], given.at[1, h], given.at[0, h])
+
+        def finish(h):
+            for i in sorted({0, half - 1}):
+                inner(h, i == 0, i == half - 1)(i)
+
+        return begin, lambda h: interior(half, inner(h)), finish
 
     def keep(buf):
         def write(h, r, value):
             buf[h, r + 1] = value
 
         return write
-
-    decode(c4, u3, s3, x3, y3, keep(b3), 2, 7, q3, g3)
-    decode(b3, u2, s2, x2, y2, keep(b2), 1, 8, q2, g2)
 
     def head(h, r, value):
         total = jnp.dot(wh[...], value, preferred_element_type=jnp.float32)
         total = total + yh[...]
         out[h, r] = total + f0[h, r + 1, :, LANES:far].astype(jnp.float32)
 
-    decode(b2, u1, s1, x1, y1, head, None, 9, q1, g1)
+    def encoder_weights(src, dst, buf):
+        arrange(src, dst, ((0, buf.shape[2]),))
+
+    def decoder_weights(src, dst, low, skip):
+        cut = low.shape[2]
+        arrange(src, dst, ((0, cut), (cut, cut + skip.shape[2])))
+
+    each = range(hours)
+    inner_one, outer_one = encoder(f0, w1, v1, s1, p1, 0)
+    inner_two, outer_two = encoder(p1, w2, v2, s2, p2, 1)
+    inner_three, outer_three = encoder(p2, w3, v3, s3, p3, 2)
+    begin_three, center_three, finish_three = decoder(
+        c4, u3, s3, x3, y3, keep(b3), 2, q3, g3
+    )
+    begin_two, center_two, finish_two = decoder(b3, u2, s2, x2, y2, keep(b2), 1, q2, g2)
+    begin_one, center_one, finish_one = decoder(b2, u1, s1, x1, y1, head, None, q1, g1)
+
+    encoder_weights(k1, w1, f0)
+    for src, dst in zip((o1, o2, o3, oc, e3, e2, e1, he), (v1, v2, v3, vc, y3, y2, y1, yh)):
+        upright(src, dst)
+    corners = []
+    for h in each:
+        wait_sides[h]()
+        for start in (0, far):
+            lanes_of = pl.ds(start, LANES)
+            corners.append(
+                vertical(
+                    f0.at[h, 1, :, lanes_of],
+                    f0.at[h, rows, :, lanes_of],
+                    f0.at[h, rows + 1, :, lanes_of],
+                    f0.at[h, 0, :, lanes_of],
+                )
+            )
+    for h in each:
+        inner_one(h)
+    encoder_weights(k2, w2, p1)
+    waits = []
+    for h in each:
+        wait_rows[h]()
+        corners[2 * h]()
+        corners[2 * h + 1]()
+        waits.append(outer_one(h))
+    encoder_weights(k3, w3, p2)
+    encoder_weights(kc, wc, p3)
+    decoder_weights(d1, x1, b2, s1)
+
+    def after(waits, work):
+        made = []
+        for h in each:
+            waits[h]()
+            made.append(work(h))
+        return made
+
+    def second(h):
+        inner_two(h)
+        return outer_two(h)
+
+    def third(h):
+        inner_three(h)
+        return outer_three(h)
+
+    def fourth(h):
+        for r in range(c4.shape[1] - 2):
+            (c4[h, r + 1],) = conv(wc, vc, taps(p3, h, r, 3), 3)
+        return begin_three(h)
+
+    def fifth(h):
+        finish_three(h)
+        return begin_two(h)
+
+    def sixth(h):
+        finish_two(h)
+        return begin_one(h)
+
+    waits = after(waits, second)
+    decoder_weights(d2, x2, b3, s2)
+    waits = after(waits, third)
+    decoder_weights(d3, x3, c4, s3)
+    wh[...] = turned(hk[...])
+    waits = after(waits, fourth)
+    for h in each:
+        center_three(h)
+    waits = after(waits, fifth)
+    for h in each:
+        center_two(h)
+    waits = after(waits, sixth)
+    for h in each:
+        center_one(h)
+    after(waits, finish_one)
 
 
 def narrow(depth, size):
@@ -464,7 +512,7 @@
         scratch_shapes=[pltpu.VMEM(shape, jnp.bfloat16) for shape in shapes]
         + [pltpu.VMEM((n, 1), jnp.float32) for n in columns]
         + [pltpu.VMEM(shape, jnp.bfloat16) for shape in sums]
-        + [pltpu.SemaphoreType.DMA((20,)), pltpu.SemaphoreType.DMA((20,))],
+        + [pltpu.SemaphoreType.DMA((20 * hours,))] * 2,
         compiler_params=pltpu.CompilerParams(
             collective_id=0, has_side_effects=True, vmem_limit_bytes=56 * 2**20
         ),

time: 85.4 us -> 74.5 us (0.87); the launches traced: 85.2 us -> 73.4 us
  Pallas kernels: 76.4 us -> 64.6 us
    pallas_call x1, Pallas kernels: 76.4 us -> 64.6 us  [body(): pl.pallas_call(functools.partial(kernel, (nty, ntx)), out_shape=jax.Shape...]
where the time goes in v4:
time: 74.5 us; the launch traced here: 73.4 us
  Pallas kernels  64.6 us (87%)
  local copies, waits for them, and re-layouts  8.79 us (12%)
    pallas_call x1, Pallas kernels, body(): pl.pallas_call(functools.partial(kernel, (nty, ntx)), out_shape=jax.Shape...  64.6 us
    transpose x1, local copies, waits for them, and re-layouts, body(): return jnp.transpose(result, (0, 2, 1, 3))  5.38 us
    unnamed x1, local copies, waits for them, and re-layouts  3.41 us

profile of v4, /device:TPU:16, one launch (start us, length us, event | category | flops | bytes accessed | tf_op | source)
XLA Modules:
  0.0 73.4 jit_solution(1871470885121752195)
XLA Ops:
  0.0 3.4 %copy.21 = bf16[2,48,8,1024]{3,1,2,0:T(8,128)(2,1)} copy(bf16[2,48,8,1024]{3,2,1,0:T(8,128)(2,1)} %param.17) | data formatting | bytes 3145728 | tf_op args[0]
  3.4 64.6 %shard_map.163 = f32[2,8,48,1024]{3,2,1,0:T(8,128)} custom-call(bf16[2,8,48,1024]{3,2,1,0:T(8,128)(2,1)} %bitcast.8, bf16[3,3,32,48]{3,2,1,0:T(8,128)(2,1)} %bitcast.10, f32[32]{0:T(128)} %o1.1, bf16[3,3,32,64]{3,2,1,0:T(8,128)(2,1)} %k2.1, f32[64]{0:T(128)} %o2.1, bf16[3,3,64,128]{3,2,1,0:T(8,128)(2,1)} %k3.1, f32[128]{0:T(128)} %o3.1, ...), custom_call_target="tpu_custom_call" | custom-call | tf_op jit(solution)/shard_map/pallas_call | solution.py:507
  68.0 5.4 %copy.19 = f32[2,48,8,1024]{3,2,1,0:T(8,128)} copy(f32[2,48,8,1024]{3,1,2,0:T(8,128)} %bitcast.7) | data formatting | bytes 6291456 | tf_op jit(solution)/shard_map/transpose | solution.py:520

commit v5 on v4

--- a/solution.py
+++ b/solution.py
@@ -337,6 +337,19 @@
 
         def begin(h):
             widen(low, up, h, 1, last + 1)
+            n, m, size = up.shape[2], skip.shape[2], offset.shape[0]
+            if n % LANES == 0 and m % LANES == 0:
+                for at, r, s in ((0, last, end), (1, 1, 1)):
+                    band = slice(3 * size * at, 3 * size * (at + 1))
+                    first, other = 3 * n * at, 4 * n + 3 * m * at
+                    taken = jnp.concatenate(
+                        (weights[band, first : first + n], weights[band, other : other + m]),
+                        axis=1,
+                    )
+                    row = jnp.concatenate((up[h, r], skip[h, s]), axis=0)
+                    (total,) = combined(taken, size, row, lanes)
+                    sums[at, h] = total.astype(jnp.bfloat16)
+                return vertical(sums.at[1, h], sums.at[0, h], given.at[1, h], given.at[0, h])
             blank, empty = jnp.zeros_like(up[h, 1]), jnp.zeros_like(skip[h, 1])
             operand = jnp.concatenate(
                 (up[h, last], blank, blank, up[h, 1])

time: 74.5 us -> 73.2 us (0.983)
  Pallas kernels: 64.6 us -> 63.5 us
    pallas_call x1, Pallas kernels: 64.6 us -> 63.5 us  [body(): pl.pallas_call(functools.partial(kernel, (nty, ntx)), out_shape=jax.Shape...]
where the time goes in v5:
time: 73.2 us; the launch traced here: 72.3 us
  Pallas kernels  63.5 us (87%)
  local copies, waits for them, and re-layouts  8.79 us (12%)
    pallas_call x1, Pallas kernels, body(): pl.pallas_call(functools.partial(kernel, (nty, ntx)), out_shape=jax.Shape...  63.5 us
    transpose x1, local copies, waits for them, and re-layouts, body(): return jnp.transpose(result, (0, 2, 1, 3))  5.38 us
    unnamed x1, local copies, waits for them, and re-layouts  3.41 us

profile of v5, /device:TPU:16, one launch (start us, length us, event | category | flops | bytes accessed | tf_op | source)
XLA Modules:
  0.0 72.3 jit_solution(1942307115677422039)
XLA Ops:
  0.0 3.4 %copy.21 = bf16[2,48,8,1024]{3,1,2,0:T(8,128)(2,1)} copy(bf16[2,48,8,1024]{3,2,1,0:T(8,128)(2,1)} %param.17) | data formatting | bytes 3145728 | tf_op args[0]
  3.4 63.5 %shard_map.163 = f32[2,8,48,1024]{3,2,1,0:T(8,128)} custom-call(bf16[2,8,48,1024]{3,2,1,0:T(8,128)(2,1)} %bitcast.8, bf16[3,3,32,48]{3,2,1,0:T(8,128)(2,1)} %bitcast.10, f32[32]{0:T(128)} %o1.1, bf16[3,3,32,64]{3,2,1,0:T(8,128)(2,1)} %k2.1, f32[64]{0:T(128)} %o2.1, bf16[3,3,64,128]{3,2,1,0:T(8,128)(2,1)} %k3.1, f32[128]{0:T(128)} %o3.1, ...), custom_call_target="tpu_custom_call" | custom-call | tf_op jit(solution)/shard_map/pallas_call | solution.py:520
  66.9 5.4 %copy.19 = f32[2,48,8,1024]{3,2,1,0:T(8,128)} copy(f32[2,48,8,1024]{3,1,2,0:T(8,128)} %bitcast.7) | data formatting | bytes 6291456 | tf_op jit(solution)/shard_map/transpose | solution.py:533
